TPU v7x, 256 devices: a whole 4x4x8 slice. The times are simulated.
256 devices in a mesh: band: 32 (over x_lo, z, core), grid: 8 (over x_hi, y).
Axes of the slice: x: 4 (x_hi: 2, x_lo: 2; x = x_hi * 2 + x_lo), y: 4, z: 8, core: 2. Of those that a mesh axis runs over, the one named last changes fastest.
Arguments:
- bands: float32 [64, 120, 14400], P('band', 'grid'), may hold values from -6 to 6
- occupations: float32 [64], P('band'), may hold values from 0.2 to 1
Outputs:
- exchange_term: float32 [64, 120, 14400], P('band', 'grid')
All inputs are finite; a program needn't handle non-finite values.
Results may differ from a plain program's by a relative error of at most 0.02.
Values may be sent and summed in bfloat16 or wider, within the bound.
A program may use at most 64 MiB of HBM per device.

v0:
```python
import math

import jax
import jax.numpy as jnp
from jax import lax
from jax.sharding import PartitionSpec as P

COULOMB = 160.0


def from_behind(block, axis, distance):
    devices = range(lax.axis_size(axis))
    route = [((i - distance) % len(devices), i) for i in devices]
    return lax.ppermute(block, axis, route)


def cas_matrix(points):
    indices = jnp.arange(points, dtype=jnp.int32)
    product = indices[:, None] * indices[None, :] % points
    phases = product.astype(jnp.float32) * (2.0 * math.pi / points)
    return ((jnp.cos(phases) + jnp.sin(phases)) / math.sqrt(points)).astype(jnp.bfloat16)


def frequency(indices, points):
    folded = jnp.where(indices <= points // 2, indices, indices - points).astype(jnp.float32)
    return folded * folded


def coulomb(first_sq, second_sq, third_sq):
    squared = first_sq[:, None, None] + second_sq[None, :, None] + third_sq[None, None, :]
    return jnp.where(squared > 0.5, COULOMB / jnp.maximum(squared, 1.0), 0.0)


def apply_third(values, matrix):
    return jnp.einsum("pxyz,kz->pxyk", values, matrix, preferred_element_type=jnp.float32)


def apply_second(values, matrix):
    return jnp.einsum("pxyz,ky->pxkz", values, matrix, preferred_element_type=jnp.float32)


def apply_first(values, matrix):
    return jnp.einsum("pxyz,kx->pkyz", values, matrix, preferred_element_type=jnp.float32)


def per_device(bands, occupations):
    members, planes, surface = bands.shape
    groups_grid = lax.axis_size("grid")
    points = planes * groups_grid
    pairs = members * members
    partner, partner_occ = from_behind((bands, occupations), "band", 1)
    hartley = cas_matrix(points)
    density = (bands[:, None] * partner[None, :]).astype(jnp.bfloat16)
    density = density.reshape(pairs, planes, points, points)
    spectrum = apply_third(density, hartley).astype(jnp.bfloat16)
    spectrum = apply_second(spectrum, hartley).astype(jnp.bfloat16)
    squares_axis = frequency(jnp.arange(points, dtype=jnp.int32), points)
    rows_each = points // groups_grid
    first_row = lax.axis_index("grid") * rows_each
    row_squares = frequency(first_row + jnp.arange(rows_each, dtype=jnp.int32), points)
    kernel_pencil = coulomb(squares_axis, row_squares, squares_axis)
    piece = lax.all_to_all(
        spectrum.reshape(pairs, planes, surface), "grid", split_axis=2, concat_axis=1, tiled=True
    )
    entries = piece.shape[0]
    pencil = piece.reshape(entries, points, rows_each, points)
    forward = apply_first(pencil, hartley).astype(jnp.bfloat16)
    scaled = (forward.astype(jnp.float32) * kernel_pencil).astype(jnp.bfloat16)
    inverse = apply_first(scaled, hartley).astype(jnp.bfloat16)
    inverse = inverse.reshape(entries, points, rows_each * points)
    mixed = lax.all_to_all(inverse, "grid", split_axis=1, concat_axis=2, tiled=True)
    mixed = mixed.reshape(pairs, planes, points, points)
    mixed = apply_second(mixed, hartley).astype(jnp.bfloat16)
    potential = apply_third(mixed, hartley)
    potential = potential.reshape(members, members, planes, surface)
    local_term = -jnp.sum(potential * (partner_occ[None, :, None, None] * partner[None]), axis=1)
    partner_term = -jnp.sum(potential * (occupations[:, None, None, None] * bands[:, None]), axis=0)
    returned = from_behind(partner_term.astype(jnp.bfloat16), "band", -1).astype(partner_term.dtype)
    return local_term + returned


def solution(mesh):
    return jax.shard_map(
        per_device,
        mesh=mesh,
        in_specs=(P("band", "grid", None), P("band")),
        out_specs=P("band", "grid", None),
        check_vma=False,
    )
```

profile of v0, /device:TPU:24, one launch (start us, length us, event | category | flops | bytes accessed | tf_op | source)
XLA Modules:
  0.0 227.8 jit_solution(12753524428971619154)
XLA Ops:
  0.0 2.0 collective-permute-start.1
  2.0 24.2 %collective-permute-done = f32[2,15,14400]{2,0,1:T(2,128)S(1)} collective-permute-done((f32[2,15,14400]{2,0,1:T(2,128)}, f32[2,15,14400]{2,0,1:T(2,128)S(1)}, u32[]{:S(2)}, u32[]{:S(2)}) %collective-permute-start) | collective-permute-done | bytes 1728032 | tf_op jit(solution)/shard_map/ppermute | solution.py:14
  26.3 1.2 copy-done.1
  27.5 4.1 %multiply_convert_fusion.1 = bf16[2,2,15,14400]{3,1,0,2:T(2,128)(2,1)} fusion(f32[2,15,14400]{2,0,1:T(2,128)S(1)} %collective-permute-done, f32[2,15,14400]{2,0,1:T(2,128)} %param.2), kind=kLoop, calls=%fused_computation.3 | loop fusion | flops 1728000 | bytes 5184000 | tf_op jit(solution)/shard_map/convert_element_type | solution.py:53
  31.6 6.3 %convert_element_type.97 = bf16[4,15,120,120]{3,2,0,1:T(8,128)(2,1)S(1)} reshape(bf16[2,2,15,14400]{3,1,0,2:T(2,128)(2,1)} %multiply_convert_fusion.1) | data formatting | bytes 3456000 | tf_op jit(solution)/shard_map/convert_element_type | solution.py:53
  37.9 2.8 %convert_bitcast_fusion.2 = bf16[4,15,120,120]{3,2,1,0:T(8,128)(2,1)} fusion(bf16[4,15,120,120]{3,2,0,1:T(8,128)(2,1)S(1)} %convert_element_type.97), kind=kOutput, calls=%fused_computation.16 | convolution fusion | flops 416793600 | bytes 3456000 | tf_op jit(solution)/shard_map/pxyz,ky->pxkz/dot_general | solution.py:39
  40.7 13.9 %copy.39 = bf16[4,15,120,120]{1,0,3,2:T(4,128)(2,1)} copy(bf16[4,15,120,120]{3,2,1,0:T(8,128)(2,1)} %convert_bitcast_fusion.2) | data formatting | bytes 3456000 | tf_op jit(solution)/shard_map/reshape | solution.py:63
  54.6 21.4 %reshape.107 = bf16[8,2,54000]{2,1,0:T(2,128)(2,1)} reshape(bf16[14400,4,15]{2,1,0:T(4,128)(2,1)} %bitcast.44) | data formatting | bytes 3456000
  75.9 7.0 %all-to-all-start = ((bf16[8,2,54000]{2,1,0:T(2,128)(2,1)}), bf16[8,2,54000]{2,1,0:T(2,128)(2,1)S(1)}, u32[]{:S(2)}, u32[]{:S(2)}) async-start(bf16[8,2,54000]{2,1,0:T(2,128)(2,1)} %reshape.107), calls=%async_computation | async-start | bytes 3457024 | tf_op jit(solution)/shard_map/all_to_all | solution.py:62
  82.9 1.9 broadcast_multiply_fusion
  84.9 1.2 fusion.30
  86.1 14.4 %all-to-all-done = bf16[8,2,54000]{2,1,0:T(2,128)(2,1)S(1)} async-done(((bf16[8,2,54000]{2,1,0:T(2,128)(2,1)}), bf16[8,2,54000]{2,1,0:T(2,128)(2,1)S(1)}, u32[]{:S(2)}, u32[]{:S(2)}) %all-to-all-start) | async-done | bytes 1728032 | tf_op jit(solution)/shard_map/all_to_all | solution.py:62
  100.5 23.6 %reshape.108 = bf16[14400,4,15]{2,1,0:T(4,128)(2,1)} reshape(bf16[8,2,54000]{2,1,0:T(2,128)(2,1)S(1)} %all-to-all-done) | data formatting | bytes 3456000
  124.1 15.7 %copy.38 = bf16[4,15,8,1800]{3,2,0,1:T(8,128)(2,1)S(1)} copy(bf16[4,15,8,1800]{1,0,3,2:T(4,128)(2,1)} %bitcast.45) | data formatting | bytes 3456000 | tf_op jit(solution)/shard_map/all_to_all | solution.py:62
  139.8 2.0 copy.27
  141.8 5.7 %reshape.101 = bf16[4,120,15,120]{3,2,0,1:T(8,128)(2,1)S(1)} reshape(bf16[4,8,15,1800]{3,0,2,1:T(4,128)(2,1)} %copy.27) | data formatting | bytes 3456000 | tf_op jit(solution)/shard_map/reshape | solution.py:66
  147.5 3.8 %convert_bitcast_fusion.1 = bf16[4,120,15,120]{3,1,2,0:T(8,128)(2,1)} fusion(f32[120,15,120]{2,0,1:T(8,128)S(1)} %copy-done.2, bf16[4,120,15,120]{3,2,0,1:T(8,128)(2,1)S(1)} %reshape.101), kind=kOutput, calls=%fused_computation.13 | convolution fusion | flops 419385600 | bytes 4320000 | tf_op jit(solution)/shard_map/pxyz,kx->pkyz/dot_general | solution.py:43
  151.4 2.8 %copy.29 = bf16[4,120,15,120]{1,3,2,0:T(8,128)(2,1)S(1)} copy(bf16[4,120,15,120]{3,1,2,0:T(8,128)(2,1)} %convert_bitcast_fusion.1) | data formatting | bytes 3456000 | tf_op jit(solution)/shard_map/convert_element_type | solution.py:69
  154.1 3.2 %copy.30 = bf16[4,120,1800]{2,0,1:T(4,128)(2,1)} copy(bf16[4,120,1800]{1,2,0:T(8,128)(2,1)S(1)} %bitcast.47) | data formatting | bytes 3456000 | tf_op jit(solution)/shard_map/reshape | solution.py:70
  157.3 5.3 %all-to-all-start.1 = ((bf16[4,120,1800]{2,0,1:T(4,128)(2,1)}), bf16[4,120,1800]{2,0,1:T(4,128)(2,1)S(1)}, u32[]{:S(2)}, u32[]{:S(2)}) async-start(bf16[4,120,1800]{2,0,1:T(4,128)(2,1)} %copy.30), calls=%async_computation.1 | async-start | bytes 3686400 | tf_op jit(solution)/shard_map/all_to_all | solution.py:71
  162.6 3.3 %broadcast_multiply_fusion.1 = f32[2,15,14400]{2,0,1:T(2,128)} fusion(f32[2,15,14400]{2,0,1:T(2,128)} %copy-done.1, f32[2]{0:T(128)S(1)} %collective-permute-done.1), kind=kLoop, calls=%fused_computation.26 | loop fusion | flops 432000 | bytes 3456008 | tf_op jit(solution)/shard_map/mul | solution.py:76
  165.9 19.1 %all-to-all-done.1 = bf16[4,120,1800]{2,0,1:T(4,128)(2,1)S(1)} async-done(((bf16[4,120,1800]{2,0,1:T(4,128)(2,1)}), bf16[4,120,1800]{2,0,1:T(4,128)(2,1)S(1)}, u32[]{:S(2)}, u32[]{:S(2)}) %all-to-all-start.1) | async-done | bytes 1728032 | tf_op jit(solution)/shard_map/all_to_all | solution.py:71
  185.0 1.4 copy.31
  186.4 5.0 %reshape.103 = bf16[4,15,120,120]{3,2,1,0:T(8,128)(2,1)S(1)} reshape(bf16[4,15,8,1800]{3,2,1,0:T(8,128)(2,1)} %copy.31) | data formatting | bytes 3456000 | tf_op jit(solution)/shard_map/reshape | solution.py:72
  191.5 0.9 convert_bitcast_fusion
  192.3 2.7 %fusion.3 = f32[4,15,120,120]{3,2,0,1:T(8,128)} fusion(bf16[4,15,120,120]{3,2,1,0:T(8,128)(2,1)S(1)} %convert_bitcast_fusion), kind=kOutput, calls=%fused_computation.6 | convolution fusion | flops 207532800 | bytes 5184000 | tf_op jit(solution)/shard_map/pxyz,kz->pxyk/dot_general | solution.py:35
  195.0 6.0 %reshape.104 = f32[2,2,15,14400]{3,1,0,2:T(2,128)S(1)} reshape(f32[4,15,120,120]{3,2,0,1:T(8,128)} %fusion.3) | data formatting | bytes 6912000 | tf_op jit(solution)/shard_map/reshape | solution.py:75
  201.0 10.1 %multiply_reduce_fusion.1 = (f32[2,15,14400]{2,0,1:T(2,128)S(1)}, f32[2,15,14400]{2,0,1:T(2,128)S(1)}) fusion(f32[2,2,15,14400]{3,1,0,2:T(2,128)S(1)} %reshape.104, f32[2,15,14400]{2,0,1:T(2,128)} %broadcast_multiply_fusion.1, f32[2,15,14400]{2,0,1:T(2,128)} %broadcast_multiply_fusion), kind=kLoop, calls=%fused_computation.2 | loop fusion | flops 2592000 | bytes 10368000 | tf_op jit(solution)/shard_map/reduce_sum | solution.py:76
  211.2 0.8 negate_convert_fusion
  212.0 3.0 %collective-permute-start.2 = (bf16[2,15,14400]{2,0,1:T(2,128)(2,1)S(1)}, bf16[2,15,14400]{2,0,1:T(2,128)(2,1)S(1)}, u32[]{:S(2)}, u32[]{:S(2)}) collective-permute-start(bf16[2,15,14400]{2,0,1:T(2,128)(2,1)S(1)} %negate_convert_fusion), channel_id=1, source_target_pairs={{8,0},{16,8},{24,16},{32,24},{40,32},{48,40},{56,48},{64,56},{72,6... | collective-permute-start | bytes 2592008 | tf_op jit(solution)/shard_map/ppermute | solution.py:14
  215.0 10.4 %collective-permute-done.2 = bf16[2,15,14400]{2,0,1:T(2,128)(2,1)S(1)} collective-permute-done((bf16[2,15,14400]{2,0,1:T(2,128)(2,1)S(1)}, bf16[2,15,14400]{2,0,1:T(2,128)(2,1)S(1)}, u32[]{:S(2)}, u32[]{:S(2)}) %collective-permute-start.2) | collective-permute-done | bytes 864032 | tf_op jit(solution)/shard_map/ppermute | solution.py:14
  225.4 2.4 %convert_add_fusion = f32[2,15,14400]{2,0,1:T(2,128)} fusion(bf16[2,15,14400]{2,0,1:T(2,128)(2,1)S(1)} %collective-permute-done.2, f32[2,15,14400]{2,0,1:T(2,128)S(1)} %get-tuple-element.5), kind=kLoop, calls=%fused_computation.19 | loop fusion | flops 1296000 | bytes 4320000 | tf_op jit(solution)/shard_map/add | solution.py:79
  (12 shorter events, 0.1 us)
Async XLA Ops:
  0.0 26.3 %collective-permute-start = (f32[2,15,14400]{2,0,1:T(2,128)}, f32[2,15,14400]{2,0,1:T(2,128)S(1)}, u32[]{:S(2)}, u32[]{:S(2)}) collective-permute-start(f32[2,15,14400]{2,0,1:T(2,128)} %param.2), channel_id=1, source_target_pairs={{248,0},{0,8},{8,16},{16,24},{24,32},{32,40},{40,48},{48,56},{56,6... | collective-permute-start | bytes 5184008 | tf_op jit(solution)/shard_map/ppermute | solution.py:14
  0.0 162.6 %collective-permute-start.1 = (f32[2]{0:T(128)}, f32[2]{0:T(128)S(1)}, u32[]{:S(2)}, u32[]{:S(2)}) collective-permute-start(f32[2]{0:T(128)} %param.3), channel_id=1, source_target_pairs={{248,0},{0,8},{8,16},{16,24},{24,32},{32,40},{40,48},{48,56},{56,6... | collective-permute-start | bytes 32 | tf_op jit(solution)/shard_map/ppermute | solution.py:14
  26.3 1.2 copy-start.1
  75.9 7.0 %copy-start = (f32[2,15,14400]{2,0,1:T(2,128)S(1)}, f32[2,15,14400]{2,0,1:T(2,128)}, u32[]{:S(2)}) copy-start(f32[2,15,14400]{2,0,1:T(2,128)} %param.2) | copy-start | bytes 5184004
  75.9 7.0 %copy-start.3 = (f32[2]{0:T(128)S(1)}, f32[2]{0:T(128)}, u32[]{:S(2)}) copy-start(f32[2]{0:T(128)} %param.3) | copy-start | bytes 28
  75.9 24.6 %all-to-all-start = ((bf16[8,2,54000]{2,1,0:T(2,128)(2,1)}), bf16[8,2,54000]{2,1,0:T(2,128)(2,1)S(1)}, u32[]{:S(2)}, u32[]{:S(2)}) async-start(bf16[8,2,54000]{2,1,0:T(2,128)(2,1)} %reshape.107), calls=%async_computation | async-start | bytes 3457024 | tf_op jit(solution)/shard_map/all_to_all | solution.py:62
  141.8 5.7 %copy-start.2 = (f32[120,15,120]{2,0,1:T(8,128)S(1)}, f32[120,15,120]{2,0,1:T(8,128)}, u32[]{:S(2)}) copy-start(f32[120,15,120]{2,0,1:T(8,128)} %fusion.30) | copy-start | bytes 2592004
  157.3 27.7 %all-to-all-start.1 = ((bf16[4,120,1800]{2,0,1:T(4,128)(2,1)}), bf16[4,120,1800]{2,0,1:T(4,128)(2,1)S(1)}, u32[]{:S(2)}, u32[]{:S(2)}) async-start(bf16[4,120,1800]{2,0,1:T(4,128)(2,1)} %copy.30), calls=%async_computation.1 | async-start | bytes 3686400 | tf_op jit(solution)/shard_map/all_to_all | solution.py:71
  212.0 13.4 %collective-permute-start.2 = (bf16[2,15,14400]{2,0,1:T(2,128)(2,1)S(1)}, bf16[2,15,14400]{2,0,1:T(2,128)(2,1)S(1)}, u32[]{:S(2)}, u32[]{:S(2)}) collective-permute-start(bf16[2,15,14400]{2,0,1:T(2,128)(2,1)S(1)} %negate_convert_fusion), channel_id=1, source_target_pairs={{8,0},{16,8},{24,16},{32,24},{40,32},{48,40},{56,48},{64,56},{72,6... | collective-permute-start | bytes 2592008 | tf_op jit(solution)/shard_map/ppermute | solution.py:14
where the time goes:
time: 231 us; the launch traced here: 228 us
  local copies, waits for them, and re-layouts  108 us (47%)
  waiting for transfers between devices  68.2 us (30%)
  other arithmetic  24 us (10%)
  starting transfers between devices  17.3 us (7%)
  matrix products  10.2 us (4%)
    unnamed x10, local copies, waits for them, and re-layouts  46.2 us
    ppermute x3, waiting for transfers between devices, from_behind(): return lax.ppermute(block, axis, route)  34.6 us
    all_to_all x1, waiting for transfers between devices, per_device(): lax.all_to_all(inverse, 'grid', split_axis=1, concat_axis=2, tiled=True)  19.1 us
    all_to_all x2, local copies, waits for them, and re-layouts, per_device(): lax.all_to_all(spectrum.reshape(pairs, planes, surface), 'grid', split_ax...  17.7 us
    all_to_all x1, waiting for transfers between devices, per_device(): lax.all_to_all(spectrum.reshape(pairs, planes, surface), 'grid', split_ax...  14.4 us
    reshape x1, local copies, waits for them, and re-layouts, per_device(): spectrum.reshape(pairs, planes, surface)  13.9 us
    reduce_sum x1, other arithmetic, per_device(): jnp.sum(potential * (partner_occ[None, :, None, None] * partner[None]), a...  10.1 us
    all_to_all x1, starting transfers between devices, per_device(): lax.all_to_all(spectrum.reshape(pairs, planes, surface), 'grid', split_ax...  6.99 us
  transfers between devices with their start and end apart: 5, of which 4 were waited for; matrix products, arithmetic and copies ran while one was open for 49% of the time, Pallas kernels for 0%

commit v1 on v0

v1 whole, which is shorter than its diff:
```python
import functools
import math

import jax
import jax.numpy as jnp
import ml_dtypes
import numpy as np
from jax import lax
from jax.experimental import pallas as pl
from jax.experimental.pallas import tpu as pltpu
from jax.sharding import PartitionSpec as P

COULOMB = 160.0
NG = 120
PAD = 128
GRID = 8
PLANES = 15
MEMBERS = 2
ROWS = 32
SURFACE = NG * NG
MESH = pl.DeviceIdType.MESH
BF = jnp.bfloat16
F32 = jnp.float32


def tables():
    n = np.arange(NG)
    angle = (n[:, None] * n[None, :] % NG).astype(np.float32) * np.float32(2.0 * math.pi / NG)
    h = (np.cos(angle) + np.sin(angle)) / np.float32(math.sqrt(NG))
    padded = np.zeros((PAD, PAD), np.float32)
    padded[:NG, :NG] = h
    second = np.zeros((GRID, MEMBERS, 16, MEMBERS, PAD), np.float32)
    for p in range(MEMBERS):
        second[:, p, :PLANES, p, :NG] = h.reshape(GRID, PLANES, NG)
    second = second.reshape(GRID * ROWS, MEMBERS * PAD)
    return (
        padded.astype(ml_dtypes.bfloat16),
        second.astype(ml_dtypes.bfloat16),
        np.ascontiguousarray(second.T).astype(ml_dtypes.bfloat16),
    )


def dot(a, b):
    return jnp.dot(a, b, preferred_element_type=F32)


def square(index):
    folded = jnp.where(index <= NG // 2, index, index - NG).astype(F32)
    return folded * folded


def kernel(bands, occ, h_ref, second_ref, second_t_ref, out,
           xin, rows32, own, part, occ_mine, occ_part, coul, send, got, wide, wide2,
           back_send, back, local, ret, ret_got,
           in_sem, sh_send, sh_recv, oc_send, oc_recv, f_send, f_recv, f_own,
           b_send, b_recv, b_own, r_send, r_recv):
    me_b = lax.axis_index("band")
    me = lax.axis_index("grid")
    groups = lax.axis_size("band")
    ahead = {"band": lax.rem(me_b + 1, groups)}
    behind = {"band": lax.rem(me_b + groups - 1, groups)}

    loads = [pltpu.make_async_copy(bands.at[i], xin.at[i], in_sem.at[i]) for i in range(MEMBERS)]
    for c in loads:
        c.start()

    barrier = pltpu.get_barrier_semaphore()
    for d in range(1, GRID):
        pl.semaphore_signal(barrier, inc=1, device_id={"grid": lax.rem(me + d, GRID)}, device_id_type=MESH)
    pl.semaphore_signal(barrier, inc=1, device_id=ahead, device_id_type=MESH)
    pl.semaphore_signal(barrier, inc=1, device_id=behind, device_id_type=MESH)

    lane = lax.broadcasted_iota(jnp.int32, (PLANES, PAD), 1)
    rows32[pl.ds(NG * 16, 8 * 16), :] = jnp.zeros((8 * 16, PAD), F32)
    wide[pl.ds(NG * ROWS, 8 * ROWS), :] = jnp.zeros((8 * ROWS, PAD), F32)
    for p in range(MEMBERS):
        wide2[pl.ds(p * 16 + 15, PAD, stride=ROWS), :] = jnp.zeros((PAD, PAD), F32)
    row = lax.broadcasted_iota(jnp.int32, (8, PAD), 0)
    occ_mine[...] = jnp.where(row == 0, occ[0], occ[1])

    shifts = []
    for i in range(MEMBERS):
        loads[i].wait()
        for r in range(NG):
            tile, off = divmod(NG * r, PAD)
            a = xin[i, :, tile * PAD:(tile + 1) * PAD]
            if off > PAD - NG:
                if (tile + 2) * PAD <= SURFACE:
                    b = xin[i, :, (tile + 1) * PAD:(tile + 2) * PAD]
                else:
                    rest = SURFACE - (tile + 1) * PAD
                    b = jnp.concatenate(
                        [xin[i, :, (tile + 1) * PAD:SURFACE], jnp.zeros((PLANES, PAD - rest), F32)], axis=1)
                a = jnp.where(lane >= off, a, b)
            if off:
                a = pltpu.roll(a, PAD - off, 1)
            rows32[pl.ds(r * 16, PLANES), :] = jnp.where(lane < NG, a, 0.0)

        def to_planes(x, _, i=i):
            own[i, x] = rows32[pl.ds(x, PAD, stride=16), :].astype(BF)
            return 0
        lax.fori_loop(0, PLANES, to_planes, 0, unroll=5)
        if i == 0:
            pl.semaphore_wait(barrier, GRID + 1)
            shift = pltpu.make_async_remote_copy(
                occ_mine, occ_part, oc_send, oc_recv, device_id=ahead, device_id_type=MESH)
            shift.start()
            shifts.append(shift)
        shift = pltpu.make_async_remote_copy(
            own.at[i], part.at[i], sh_send.at[i], sh_recv.at[i], device_id=ahead, device_id_type=MESH)
        shift.start()
        shifts.append(shift)

    kx = square(lax.broadcasted_iota(jnp.int32, (PAD, PAD), 0))
    kz = square(lax.broadcasted_iota(jnp.int32, (PAD, PAD), 1))
    plane_sq = kx + kz

    def fill(l, _):
        s = plane_sq + square(me * PLANES + l)
        coul[l] = jnp.where(s > 0.5, COULOMB / jnp.maximum(s, 1.0), 0.0)
        return 0
    lax.fori_loop(0, PLANES, fill, 0)

    sends = []
    for j in range(MEMBERS):
        shifts[1 + j].wait_recv()

        def forward(x, _, j=j):
            v = part[j, x]
            d = jnp.concatenate([own[0, x] * v, own[1, x] * v], axis=0)
            t = dot(d, h_ref[...]).astype(BF)
            send[j, x] = dot(second_ref[...], t).astype(BF)
            return 0
        lax.fori_loop(0, PLANES, forward, 0, unroll=3)

        mine = pltpu.make_async_copy(
            send.at[j, :, pl.ds(pl.multiple_of(me * ROWS, ROWS), ROWS)],
            got.at[j, pl.ds(me * PLANES, PLANES)], f_own.at[j])
        mine.start()
        chunk = [mine]
        for d in range(1, GRID):
            to = lax.rem(me + d, GRID)
            c = pltpu.make_async_remote_copy(
                send.at[j, :, pl.ds(pl.multiple_of(to * ROWS, ROWS), ROWS)],
                got.at[j, pl.ds(me * PLANES, PLANES)],
                f_send.at[j, d], f_recv.at[j, d], device_id={"grid": to}, device_id_type=MESH)
            c.start()
            chunk.append(c)
        sends.append(chunk)

    backs = []
    for j in range(MEMBERS):
        sends[j][0].wait()
        for c in sends[j][1:]:
            c.wait_recv()

        def widen(x, _, j=j):
            wide[pl.ds(pl.multiple_of(x * ROWS, ROWS), ROWS), :] = got[j, x].astype(F32)
            return 0
        lax.fori_loop(0, NG, widen, 0, unroll=8)

        def solve(l, _):
            r = jnp.concatenate(
                [wide[pl.ds(l, PAD, stride=ROWS), :], wide[pl.ds(16 + l, PAD, stride=ROWS), :]], axis=1)
            f = dot(h_ref[...], r.astype(BF))
            k = coul[l]
            f = (f * jnp.concatenate([k, k], axis=1)).astype(BF)
            g = dot(h_ref[...], f)
            wide2[pl.ds(l, PAD, stride=ROWS), :] = g[:, :PAD]
            wide2[pl.ds(16 + l, PAD, stride=ROWS), :] = g[:, PAD:]
            return 0
        lax.fori_loop(0, PLANES, solve, 0, unroll=3)

        def narrow(x, _, j=j):
            back_send[j, x] = wide2[pl.ds(pl.multiple_of(x * ROWS, ROWS), ROWS), :].astype(BF)
            return 0
        lax.fori_loop(0, NG, narrow, 0, unroll=8)

        mine = pltpu.make_async_copy(
            back_send.at[j, pl.ds(me * PLANES, PLANES)],
            back.at[j, :, pl.ds(pl.multiple_of(me * ROWS, ROWS), ROWS)], b_own.at[j])
        mine.start()
        chunk = [mine]
        for d in range(1, GRID):
            to = lax.rem(me + d, GRID)
            c = pltpu.make_async_remote_copy(
                back_send.at[j, pl.ds(to * PLANES, PLANES)],
                back.at[j, :, pl.ds(pl.multiple_of(me * ROWS, ROWS), ROWS)],
                b_send.at[j, d], b_recv.at[j, d], device_id={"grid": to}, device_id_type=MESH)
            c.start()
            chunk.append(c)
        backs.append(chunk)

    shifts[0].wait_recv()
    returns = []
    for j in range(MEMBERS):
        backs[j][0].wait()
        for c in backs[j][1:]:
            c.wait_recv()

        def inverse(x, _, j=j):
            u = dot(second_t_ref[...], back[j, x]).astype(BF)
            v = dot(u, h_ref[...])
            v0, v1 = v[:PAD], v[PAD:]
            w = part[j, x].astype(F32) * occ_part[pl.ds(j, 1), :]
            row0 = pl.ds(pl.multiple_of(x * PAD, PAD), PAD)
            row1 = pl.ds(pl.multiple_of((PLANES + x) * PAD, PAD), PAD)
            if j == 0:
                local[row0, :] = -(v0 * w)
                local[row1, :] = -(v1 * w)
            else:
                local[row0, :] -= v0 * w
                local[row1, :] -= v1 * w
            q = (v0 * (own[0, x].astype(F32) * occ_mine[pl.ds(0, 1), :])
                 + v1 * (own[1, x].astype(F32) * occ_mine[pl.ds(1, 1), :]))
            ret[j, x] = (-q).astype(BF)
            return 0
        lax.fori_loop(0, PLANES, inverse, 0, unroll=3)
        c = pltpu.make_async_remote_copy(
            ret.at[j], ret_got.at[j], r_send.at[j], r_recv.at[j], device_id=behind, device_id_type=MESH)
        c.start()
        returns.append(c)

    local[pl.ds(2 * PLANES * PAD, PAD), :] = jnp.zeros((PAD, PAD), F32)
    for i in range(MEMBERS):
        returns[i].wait_recv()

        def total(x, _, i=i):
            rows = pl.ds(pl.multiple_of((i * PLANES + x) * PAD, PAD), PAD)
            local[rows, :] += ret_got[i, x].astype(F32)
            return 0
        lax.fori_loop(0, PLANES, total, 0, unroll=3)

        rolled = []
        for r in range(NG):
            tile = -(-NG * r // PAD)
            first = PAD * tile - NG * r
            v = local[pl.ds(i * PLANES * PAD + r, 16, stride=PAD), :]
            rolled.append(pltpu.roll(v, PAD - first, 1) if first else v)
            if r % 16:
                t = tile - 1
                z0 = PAD * t - NG * (r - 1)
                full = jnp.where(lane < NG - z0, rolled[r - 1][:PLANES], rolled[r][:PLANES])
                out[i, :, t * PAD:(t + 1) * PAD] = full
        out[i, :, SURFACE - 64:] = rolled[NG - 1][:PLANES, :64]

    for c in shifts:
        c.wait_send()
    for chunk in sends + backs:
        for c in chunk[1:]:
            c.wait_send()
    for c in returns:
        c.wait_send()


def per_device(bands, occupations):
    h, second, second_t = (jnp.asarray(t) for t in tables())
    dma = pltpu.SemaphoreType.DMA
    vmem = pl.BlockSpec(memory_space=pltpu.VMEM)
    return pl.pallas_call(
        kernel,
        out_shape=jax.ShapeDtypeStruct(bands.shape, F32),
        in_specs=[pl.BlockSpec(memory_space=pl.ANY), pl.BlockSpec(memory_space=pltpu.SMEM), vmem, vmem, vmem],
        out_specs=vmem,
        scratch_shapes=[
            pltpu.VMEM((MEMBERS, PLANES, SURFACE), F32),
            pltpu.VMEM((PAD * 16, PAD), F32),
            pltpu.VMEM((MEMBERS, PLANES, PAD, PAD), BF),
            pltpu.VMEM((MEMBERS, PLANES, PAD, PAD), BF),
            pltpu.VMEM((8, PAD), F32),
            pltpu.VMEM((8, PAD), F32),
            pltpu.VMEM((PLANES, PAD, PAD), F32),
            pltpu.VMEM((MEMBERS, PLANES, GRID * ROWS, PAD), BF),
            pltpu.VMEM((MEMBERS, NG, ROWS, PAD), BF),
            pltpu.VMEM((PAD * ROWS, PAD), F32),
            pltpu.VMEM((PAD * ROWS, PAD), F32),
            pltpu.VMEM((MEMBERS, NG, ROWS, PAD), BF),
            pltpu.VMEM((MEMBERS, PLANES, GRID * ROWS, PAD), BF),
            pltpu.VMEM(((2 * PLANES + 1) * PAD, PAD), F32),
            pltpu.VMEM((MEMBERS, PLANES, PAD, PAD), BF),
            pltpu.VMEM((MEMBERS, PLANES, PAD, PAD), BF),
            dma((MEMBERS,)), dma((MEMBERS,)), dma((MEMBERS,)), dma, dma,
            dma((MEMBERS, GRID)), dma((MEMBERS, GRID)), dma((MEMBERS,)),
            dma((MEMBERS, GRID)), dma((MEMBERS, GRID)), dma((MEMBERS,)),
            dma((MEMBERS,)), dma((MEMBERS,)),
        ],
        compiler_params=pltpu.CompilerParams(
            collective_id=0, has_side_effects=True, vmem_limit_bytes=48 * 2**20),
    )(bands, occupations, h, second, second_t)


def solution(mesh):
    return jax.shard_map(
        per_device,
        mesh=mesh,
        in_specs=(P("band", "grid", None), P("band")),
        out_specs=P("band", "grid", None),
        check_vma=False,
    )
```

time: 231 us -> 86.7 us (0.38)
  the two profiles are of different devices: /device:TPU:24 before, /device:TPU:28 now
where the time goes in v1:
time: 86.7 us; the launch traced here: 86.6 us
  Pallas kernels  82.7 us (95%)
  local copies, waits for them, and re-layouts  3.76 us (4%)
    pallas_call x1, Pallas kernels, per_device(): pl.pallas_call(kernel, out_shape=jax.ShapeDtypeStruct(bands.shape, F32),...  82.7 us
    pallas_call x1, local copies, waits for them, and re-layouts, per_device(): pl.pallas_call(kernel, out_shape=jax.ShapeDtypeStruct(bands.shape, F32),...  2.09 us

profile of v1, /device:TPU:28, one launch (start us, length us, event | category | flops | bytes accessed | tf_op | source)
XLA Modules:
  0.0 86.6 jit_solution(18243288547241093469)
XLA Ops:
  0.0 0.0 copy-start
  0.0 0.0 copy-start.1
  0.0 0.0 copy-start.2
  0.0 0.0 copy-start.3
  0.0 1.7 %copy.6.bands = f32[2,15,14400]{2,1,0:T(8,128)S(1)} copy(f32[2,15,14400]{2,0,1:T(2,128)} %param.5) | data formatting | bytes 3456000 | tf_op args[0]
  1.7 0.0 copy-done
  1.7 0.0 copy-done.1
  1.7 0.0 copy-done.2
  1.7 0.0 copy-done.3
  1.7 82.7 %shard_map.55 = f32[2,15,14400]{2,1,0:T(8,128)S(1)} custom-call(f32[2,15,14400]{2,1,0:T(8,128)S(1)} %copy.6.bands, f32[2]{0:T(128)S(1)} %copy-done.3, bf16[128,128]{1,0:T(8,128)(2,1)S(1)} %copy-done.2, bf16[256,256]{1,0:T(8,128)(2,1)S(1)} %copy-done.1, bf16[256,256]{1,0:T(8,128)(2,1)S(1)} %copy-done), custom_call_target="tpu_custom_call" | custom-call | tf_op jit(solution)/shard_map/pallas_call | solution.py:260
  84.5 2.1 %copy.7 = f32[2,15,14400]{2,0,1:T(2,128)} copy(f32[2,15,14400]{2,1,0:T(8,128)S(1)} %shard_map.55) | data formatting | bytes 3456000 | tf_op jit(solution)/shard_map/pallas_call | solution.py:260
Async XLA Ops:
  0.0 1.7 %copy-start = (bf16[256,256]{1,0:T(8,128)(2,1)S(1)}, bf16[256,256]{1,0:T(8,128)(2,1)}, u32[]{:S(2)}) copy-start(bf16[256,256]{1,0:T(8,128)(2,1)} %constant.8.clone.second_t_ref) | copy-start | bytes 393220
  0.0 1.7 %copy-start.1 = (bf16[256,256]{1,0:T(8,128)(2,1)S(1)}, bf16[256,256]{1,0:T(8,128)(2,1)}, u32[]{:S(2)}) copy-start(bf16[256,256]{1,0:T(8,128)(2,1)} %constant.7.clone.second_ref) | copy-start | bytes 393220
  0.0 1.7 %copy-start.2 = (bf16[128,128]{1,0:T(8,128)(2,1)S(1)}, bf16[128,128]{1,0:T(8,128)(2,1)}, u32[]{:S(2)}) copy-start(bf16[128,128]{1,0:T(8,128)(2,1)} %constant.6.clone.h_ref) | copy-start | bytes 98308
  0.0 1.7 %copy-start.3 = (f32[2]{0:T(128)S(1)}, f32[2]{0:T(128)}, u32[]{:S(2)}) copy-start(f32[2]{0:T(128)} %occ.1) | copy-start | bytes 28

commit v2 on v1

v2 whole, which is shorter than its diff:
```python
import functools
import math

import jax
import jax.numpy as jnp
import ml_dtypes
import numpy as np
from jax import lax
from jax.experimental import pallas as pl
from jax.experimental.pallas import tpu as pltpu
from jax.sharding import PartitionSpec as P

COULOMB = 160.0
NG = 120
PAD = 128
GRID = 8
PLANES = 15
MEMBERS = 2
ROWS = 32
XG = 5
NQ = PLANES // XG
SURFACE = NG * NG
MESH = pl.DeviceIdType.MESH
BF = jnp.bfloat16
F32 = jnp.float32


def tables():
    n = np.arange(NG)
    angle = (n[:, None] * n[None, :] % NG).astype(np.float32) * np.float32(2.0 * math.pi / NG)
    h = (np.cos(angle) + np.sin(angle)) / np.float32(math.sqrt(NG))
    padded = np.zeros((PAD, PAD), np.float32)
    padded[:NG, :NG] = h
    second = np.zeros((GRID, MEMBERS, 16, MEMBERS, PAD), np.float32)
    for p in range(MEMBERS):
        second[:, p, :PLANES, p, :NG] = h.reshape(GRID, PLANES, NG)
    second = second.reshape(GRID * ROWS, MEMBERS * PAD)
    return (
        padded.astype(ml_dtypes.bfloat16),
        second.astype(ml_dtypes.bfloat16),
        np.ascontiguousarray(second.T).astype(ml_dtypes.bfloat16),
    )


def dot(a, b):
    return jnp.dot(a, b, preferred_element_type=F32)


def square(index):
    folded = jnp.where(index <= NG // 2, index, index - NG).astype(F32)
    return folded * folded


def kernel(bands, occ, h_hbm, second_hbm, second_t_hbm, out,
           xin, rows32, own, part, occ_mine, occ_part, coul, send, got, wide, wide2,
           back_send, back, local, ret, ret_got, xout, h_ref, second_ref, second_t_ref,
           in_sem, c_sem, out_sem, sh_send, sh_recv, oc_send, oc_recv, f_send, f_recv, f_own,
           b_send, b_recv, b_own, r_send, r_recv):
    me_b = lax.axis_index("band")
    me = lax.axis_index("grid")
    groups = lax.axis_size("band")
    ahead = {"band": lax.rem(me_b + 1, groups)}
    behind = {"band": lax.rem(me_b + groups - 1, groups)}

    def span(q):
        return pl.ds(q * XG, XG)

    loads = [pltpu.make_async_copy(bands.at[span(q)], xin.at[span(q)], in_sem.at[q]) for q in range(NQ)]
    consts = [
        pltpu.make_async_copy(src, dst, c_sem.at[n])
        for n, (src, dst) in enumerate(
            ((h_hbm, h_ref), (second_hbm, second_ref), (second_t_hbm, second_t_ref)))
    ]
    for c in loads + consts:
        c.start()

    barrier = pltpu.get_barrier_semaphore()
    for d in range(1, GRID):
        pl.semaphore_signal(barrier, inc=1, device_id={"grid": lax.rem(me + d, GRID)}, device_id_type=MESH)
    pl.semaphore_signal(barrier, inc=1, device_id=ahead, device_id_type=MESH)
    pl.semaphore_signal(barrier, inc=1, device_id=behind, device_id_type=MESH)

    lane = lax.broadcasted_iota(jnp.int32, (MEMBERS, PAD), 1)
    rows32[pl.ds(NG * MEMBERS, 8 * MEMBERS), :] = jnp.zeros((8 * MEMBERS, PAD), F32)
    wide[pl.ds(NG * ROWS, 8 * ROWS), :] = jnp.zeros((8 * ROWS, PAD), F32)
    for p in range(MEMBERS):
        wide2[pl.ds(p * 16 + 15, PAD, stride=ROWS), :] = jnp.zeros((PAD, PAD), F32)
    row = lax.broadcasted_iota(jnp.int32, (8, PAD), 0)
    occ_mine[...] = jnp.where(row == 0, occ[0], occ[1])

    def unpack(x, _):
        tiles = {}

        def tile_of(t):
            if t not in tiles:
                if (t + 1) * PAD <= SURFACE:
                    tiles[t] = xin[x, :, t * PAD:(t + 1) * PAD]
                else:
                    half = xin[x, :, t * PAD:SURFACE]
                    tiles[t] = jnp.concatenate([half, jnp.zeros_like(half)], axis=1)
            return tiles[t]

        for r in range(NG):
            tile, off = divmod(NG * r, PAD)
            a = tile_of(tile)
            if off > PAD - NG:
                a = jnp.where(lane >= off, a, tile_of(tile + 1))
            if off:
                a = pltpu.roll(a, PAD - off, 1)
            rows32[pl.ds(r * MEMBERS, MEMBERS), :] = jnp.where(lane < NG, a, 0.0)
        for i in range(MEMBERS):
            own[i, x] = rows32[pl.ds(i, PAD, stride=MEMBERS), :].astype(BF)
        return 0

    def shift_of(j, q):
        return pltpu.make_async_remote_copy(
            own.at[j, span(q)], part.at[j, span(q)], sh_send.at[j, q], sh_recv.at[j, q],
            device_id=ahead, device_id_type=MESH)

    shifts = [[shift_of(j, q) for q in range(NQ)] for j in range(MEMBERS)]
    occ_shift = pltpu.make_async_remote_copy(
        occ_mine, occ_part, oc_send, oc_recv, device_id=ahead, device_id_type=MESH)
    for q in range(NQ):
        loads[q].wait()
        lax.fori_loop(q * XG, (q + 1) * XG, unpack, 0)
        if q == 0:
            pl.semaphore_wait(barrier, GRID + 1)
        shifts[0][q].start()
    for q in range(NQ):
        shifts[1][q].start()
    occ_shift.start()

    kx = square(lax.broadcasted_iota(jnp.int32, (PAD, PAD), 0))
    kz = square(lax.broadcasted_iota(jnp.int32, (PAD, PAD), 1))
    plane_sq = kx + kz

    def fill(l, _):
        s = plane_sq + square(me * PLANES + l)
        coul[l] = jnp.where(s > 0.5, COULOMB / jnp.maximum(s, 1.0), 0.0)
        return 0
    lax.fori_loop(0, PLANES, fill, 0)
    for c in consts:
        c.wait()

    mine_rows = pl.ds(pl.multiple_of(me * ROWS, ROWS), ROWS)
    sends = []
    for j in range(MEMBERS):
        for q in range(NQ):
            shifts[j][q].wait_recv()

            def forward(x, _, j=j):
                v = part[j, x]
                d = jnp.concatenate([own[0, x] * v, own[1, x] * v], axis=0)
                t = dot(d, h_ref[...]).astype(BF)
                send[j, x] = dot(second_ref[...], t).astype(BF)
                return 0
            lax.fori_loop(q * XG, (q + 1) * XG, forward, 0, unroll=XG)

            mine = pltpu.make_async_copy(
                send.at[j, span(q), mine_rows],
                got.at[j, pl.ds(me * PLANES + q * XG, XG)], f_own.at[j, q])
            mine.start()
            chunk = [mine]
            for d in range(1, GRID):
                to = lax.rem(me + d, GRID)
                c = pltpu.make_async_remote_copy(
                    send.at[j, span(q), pl.ds(pl.multiple_of(to * ROWS, ROWS), ROWS)],
                    got.at[j, pl.ds(me * PLANES + q * XG, XG)],
                    f_send.at[j, q, d], f_recv.at[j, q, d], device_id={"grid": to}, device_id_type=MESH)
                c.start()
                chunk.append(c)
            sends.append(chunk)

    backs = []
    for j in range(MEMBERS):
        for q in range(NQ):
            sends[j * NQ + q][0].wait()
            for c in sends[j * NQ + q][1:]:
                c.wait_recv()

        def widen(x, _, j=j):
            wide[pl.ds(pl.multiple_of(x * ROWS, ROWS), ROWS), :] = got[j, x].astype(F32)
            return 0
        lax.fori_loop(0, NG, widen, 0, unroll=8)

        def solve(l, _):
            r = jnp.concatenate(
                [wide[pl.ds(l, PAD, stride=ROWS), :], wide[pl.ds(16 + l, PAD, stride=ROWS), :]], axis=1)
            f = dot(h_ref[...], r.astype(BF))
            k = coul[l]
            f = (f * jnp.concatenate([k, k], axis=1)).astype(BF)
            g = dot(h_ref[...], f)
            wide2[pl.ds(l, PAD, stride=ROWS), :] = g[:, :PAD]
            wide2[pl.ds(16 + l, PAD, stride=ROWS), :] = g[:, PAD:]
            return 0
        lax.fori_loop(0, PLANES, solve, 0, unroll=5)

        for q in range(NQ):
            def narrow(g, _, j=j, q=q):
                for x in range(XG):
                    at = g * PLANES + q * XG + x
                    back_send[j, at] = wide2[pl.ds(pl.multiple_of(at * ROWS, ROWS), ROWS), :].astype(BF)
                return 0
            lax.fori_loop(0, GRID, narrow, 0, unroll=2)

            mine = pltpu.make_async_copy(
                back_send.at[j, pl.ds(me * PLANES + q * XG, XG)],
                back.at[j, span(q), mine_rows], b_own.at[j, q])
            mine.start()
            chunk = [mine]
            for d in range(1, GRID):
                to = lax.rem(me + d, GRID)
                c = pltpu.make_async_remote_copy(
                    back_send.at[j, pl.ds(to * PLANES + q * XG, XG)],
                    back.at[j, span(q), mine_rows],
                    b_send.at[j, q, d], b_recv.at[j, q, d], device_id={"grid": to}, device_id_type=MESH)
                c.start()
                chunk.append(c)
            backs.append(chunk)

    occ_shift.wait_recv()
    returns = []
    for j in range(MEMBERS):
        for q in range(NQ):
            backs[j * NQ + q][0].wait()
            for c in backs[j * NQ + q][1:]:
                c.wait_recv()

            def inverse(x, _, j=j):
                u = dot(second_t_ref[...], back[j, x]).astype(BF)
                v = dot(u, h_ref[...])
                v0, v1 = v[:PAD], v[PAD:]
                w = part[j, x].astype(F32) * occ_part[pl.ds(j, 1), :]
                if j == 0:
                    local[0, x] = -(v0 * w)
                    local[1, x] = -(v1 * w)
                else:
                    local[0, x] -= v0 * w
                    local[1, x] -= v1 * w
                s = (v0 * (own[0, x].astype(F32) * occ_mine[pl.ds(0, 1), :])
                     + v1 * (own[1, x].astype(F32) * occ_mine[pl.ds(1, 1), :]))
                ret[j, x] = (-s).astype(BF)
                return 0
            lax.fori_loop(q * XG, (q + 1) * XG, inverse, 0, unroll=XG)
            c = pltpu.make_async_remote_copy(
                ret.at[j, span(q)], ret_got.at[j, span(q)], r_send.at[j, q], r_recv.at[j, q],
                device_id=behind, device_id_type=MESH)
            c.start()
            returns.append(c)

    def pack(x, _):
        for i in range(MEMBERS):
            rows32[pl.ds(i, PAD, stride=MEMBERS), :] = local[i, x] + ret_got[i, x].astype(F32)
        before = None
        for r in range(NG):
            tile = -(-NG * r // PAD)
            first = PAD * tile - NG * r
            v = rows32[pl.ds(r * MEMBERS, MEMBERS), :]
            if first:
                v = pltpu.roll(v, PAD - first, 1)
            if r % 16:
                t = tile - 1
                z0 = PAD * t - NG * (r - 1)
                xout[x, :, t * PAD:(t + 1) * PAD] = jnp.where(lane < NG - z0, before, v)
            before = v
        xout[x, :, SURFACE - 64:] = before[:, :64]
        return 0

    stores = []
    for q in range(NQ):
        for j in range(MEMBERS):
            returns[j * NQ + q].wait_recv()
        lax.fori_loop(q * XG, (q + 1) * XG, pack, 0)
        c = pltpu.make_async_copy(xout.at[span(q)], out.at[span(q)], out_sem.at[q])
        c.start()
        stores.append(c)

    for c in stores:
        c.wait()
    for c in shifts[0] + shifts[1] + [occ_shift] + returns:
        c.wait_send()
    for chunk in sends + backs:
        for c in chunk[1:]:
            c.wait_send()


def per_device(bands, occupations):
    h, second, second_t = (jnp.asarray(t) for t in tables())
    dma = pltpu.SemaphoreType.DMA
    hbm = pl.BlockSpec(memory_space=pl.ANY)
    planes_first = bands.transpose(1, 0, 2)
    total = pl.pallas_call(
        kernel,
        out_shape=jax.ShapeDtypeStruct(planes_first.shape, F32),
        in_specs=[hbm, pl.BlockSpec(memory_space=pltpu.SMEM), hbm, hbm, hbm],
        out_specs=hbm,
        scratch_shapes=[
            pltpu.VMEM((PLANES, MEMBERS, SURFACE), F32),
            pltpu.VMEM((PAD * MEMBERS, PAD), F32),
            pltpu.VMEM((MEMBERS, PLANES, PAD, PAD), BF),
            pltpu.VMEM((MEMBERS, PLANES, PAD, PAD), BF),
            pltpu.VMEM((8, PAD), F32),
            pltpu.VMEM((8, PAD), F32),
            pltpu.VMEM((PLANES, PAD, PAD), F32),
            pltpu.VMEM((MEMBERS, PLANES, GRID * ROWS, PAD), BF),
            pltpu.VMEM((MEMBERS, NG, ROWS, PAD), BF),
            pltpu.VMEM((PAD * ROWS, PAD), F32),
            pltpu.VMEM((PAD * ROWS, PAD), F32),
            pltpu.VMEM((MEMBERS, NG, ROWS, PAD), BF),
            pltpu.VMEM((MEMBERS, PLANES, GRID * ROWS, PAD), BF),
            pltpu.VMEM((MEMBERS, PLANES, PAD, PAD), F32),
            pltpu.VMEM((MEMBERS, PLANES, PAD, PAD), BF),
            pltpu.VMEM((MEMBERS, PLANES, PAD, PAD), BF),
            pltpu.VMEM((PLANES, MEMBERS, SURFACE), F32),
            pltpu.VMEM(h.shape, BF),
            pltpu.VMEM(second.shape, BF),
            pltpu.VMEM(second_t.shape, BF),
            dma((NQ,)), dma((3,)), dma((NQ,)),
            dma((MEMBERS, NQ)), dma((MEMBERS, NQ)), dma, dma,
            dma((MEMBERS, NQ, GRID)), dma((MEMBERS, NQ, GRID)), dma((MEMBERS, NQ)),
            dma((MEMBERS, NQ, GRID)), dma((MEMBERS, NQ, GRID)), dma((MEMBERS, NQ)),
            dma((MEMBERS, NQ)), dma((MEMBERS, NQ)),
        ],
        compiler_params=pltpu.CompilerParams(
            collective_id=0, has_side_effects=True, vmem_limit_bytes=58 * 2**20),
    )(planes_first, occupations, h, second, second_t)
    return total.transpose(1, 0, 2)


def solution(mesh):
    return jax.shard_map(
        per_device,
        mesh=mesh,
        in_specs=(P("band", "grid", None), P("band")),
        out_specs=P("band", "grid", None),
        check_vma=False,
    )
```

time: 86.7 us -> 76 us (0.88)
  the two profiles are of different devices: /device:TPU:28 before, /device:TPU:24 now
where the time goes in v2:
time: 76 us; the launch traced here: 75.8 us
  Pallas kernels  73 us (96%)
  local copies, waits for them, and re-layouts  2.78 us (4%)
    pallas_call x1, Pallas kernels, per_device(): pl.pallas_call(kernel, out_shape=jax.ShapeDtypeStruct(planes_first.shape,...  73 us
    unnamed x1, local copies, waits for them, and re-layouts  2.78 us

profile of v2, /device:TPU:24, one launch (start us, length us, event | category | flops | bytes accessed | tf_op | source)
XLA Modules:
  0.0 75.8 jit_solution(13385706665396359119)
XLA Ops:
  0.0 73.0 %shard_map.55 = f32[15,2,14400]{2,1,0:T(2,128)} custom-call(f32[15,2,14400]{2,1,0:T(2,128)} %bitcast.3, f32[2]{0:T(128)} %occ.1, bf16[128,128]{1,0:T(8,128)(2,1)} %constant.6.clone.h_hbm, bf16[256,256]{1,0:T(8,128)(2,1)} %constant.7.clone.second_hbm, bf16[256,256]{1,0:T(8,128)(2,1)} %constant.8.clone.second_t_hbm), custom_call_target="tpu_custom_call" | custom-call | tf_op jit(solution)/shard_map/pallas_call | solution.py:292
  73.0 2.8 %copy.7 = f32[2,15,14400]{2,0,1:T(2,128)} copy(f32[2,15,14400]{2,0,1:T(2,128)} %bitcast.2) | data formatting | bytes 3456000

commit v3 on v2

v3 whole, which is shorter than its diff:
```python
import functools
import math

import jax
import jax.numpy as jnp
import ml_dtypes
import numpy as np
from jax import lax
from jax.experimental import pallas as pl
from jax.experimental.pallas import tpu as pltpu
from jax.sharding import PartitionSpec as P

COULOMB = 160.0
NG = 120
PAD = 128
GRID = 8
PLANES = 15
MEMBERS = 2
ROWS = 32
TILE = 16
OUT_GROUPS = ((0, 5), (5, 5), (10, 5))
BACK_GROUPS = ((0, 5), (5, 5), (10, 5))
NQ = len(OUT_GROUPS)
RELAY_Z = {1: 6, 2: 5}
RELAY_PLANES = max(OUT_GROUPS[q][1] for q in RELAY_Z)
SURFACE = NG * NG
MESH = pl.DeviceIdType.MESH
BF = jnp.bfloat16
F32 = jnp.float32


def tables():
    n = np.arange(NG)
    angle = (n[:, None] * n[None, :] % NG).astype(np.float32) * np.float32(2.0 * math.pi / NG)
    h = (np.cos(angle) + np.sin(angle)) / np.float32(math.sqrt(NG))
    padded = np.zeros((PAD, PAD), np.float32)
    padded[:NG, :NG] = h
    second = np.zeros((GRID * ROWS, MEMBERS, PAD), np.float32)
    for p in range(MEMBERS):
        second[p * NG:(p + 1) * NG, p, :NG] = h
    second = second.reshape(GRID * ROWS, MEMBERS * PAD)
    return (
        padded.astype(ml_dtypes.bfloat16),
        second.astype(ml_dtypes.bfloat16),
        np.ascontiguousarray(second.T).astype(ml_dtypes.bfloat16),
    )


def dot(a, b):
    return jnp.dot(a, b, preferred_element_type=F32)


def square(index):
    folded = jnp.where(index <= NG // 2, index, index - NG).astype(F32)
    return folded * folded


def kernel(bands, occ, h_hbm, second_hbm, second_t_hbm, out,
           xin, rows32, own, part, occ_mine, occ_part, coul, send, got, wide, wide2,
           back_send, back, local, ret, ret_got, xout, h_ref, second_ref, second_t_ref, relayed,
           in_sem, c_sem, out_sem, sh_send, sh_recv, oc_send, oc_recv, f_send, f_recv, f_own,
           b_send, b_recv, b_own, r_send, r_recv, re_send, re_recv):
    me_b = lax.axis_index("band")
    me = lax.axis_index("grid")
    groups = lax.axis_size("band")
    core = lax.rem(me_b, 2)
    ahead = {"band": lax.rem(me_b + 1, groups)}
    behind = {"band": lax.rem(me_b + groups - 1, groups)}

    side = groups // 2
    column = me_b // side
    place = lax.rem(me_b, side)
    first = place == 0
    last = place == side - 1
    other = (1 - column) * side

    def remote(src, dst, send_sem, recv_sem, to):
        return pltpu.make_async_remote_copy(
            src, dst, send_sem, recv_sem, device_id=to, device_id_type=MESH)

    def out_span(q):
        return pl.ds(*OUT_GROUPS[q])

    def back_span(q):
        return pl.ds(*BACK_GROUPS[q])

    loads = [
        pltpu.make_async_copy(bands.at[out_span(q)], xin.at[out_span(q)], in_sem.at[q]) for q in range(NQ)]
    consts = [
        pltpu.make_async_copy(src, dst, c_sem.at[n])
        for n, (src, dst) in enumerate(
            ((h_hbm, h_ref), (second_hbm, second_ref), (second_t_hbm, second_t_ref)))
    ]
    for c in loads + consts:
        c.start()

    def greet(to):
        pl.semaphore_signal(barrier, inc=1, device_id=to, device_id_type=MESH)

    barrier = pltpu.get_barrier_semaphore()
    for d in range(1, GRID):
        greet({"grid": lax.rem(me + d, GRID)})
    greet(ahead)
    greet(behind)
    greetings = GRID + 1 + jnp.where(last, len(RELAY_Z), 0)
    for z in RELAY_Z.values():
        @pl.when(place == 2 * z + 1)
        def _():
            greet({"band": other + side - 1})

        @pl.when(first)
        def _(z=z):
            greet({"band": column * side + 2 * z + 1})
        greetings += (place == 2 * z + 1).astype(jnp.int32)

    lane = lax.broadcasted_iota(jnp.int32, (MEMBERS, PAD), 1)
    rows32[pl.ds(NG * MEMBERS, 8 * MEMBERS), :] = jnp.zeros((8 * MEMBERS, PAD), F32)
    wide[pl.ds(NG * ROWS, 8 * ROWS), :] = jnp.zeros((8 * ROWS, PAD), F32)
    row = lax.broadcasted_iota(jnp.int32, (8, PAD), 0)
    occ_mine[...] = jnp.where(row == 0, occ[0], occ[1])

    def unpack(x, _):
        tiles = {}

        def tile_of(t):
            if t not in tiles:
                if (t + 1) * PAD <= SURFACE:
                    tiles[t] = xin[x, :, t * PAD:(t + 1) * PAD]
                else:
                    half = xin[x, :, t * PAD:SURFACE]
                    tiles[t] = jnp.concatenate([half, jnp.zeros_like(half)], axis=1)
            return tiles[t]

        for r in range(NG):
            tile, off = divmod(NG * r, PAD)
            a = tile_of(tile)
            if off > PAD - NG:
                a = jnp.where(lane >= off, a, tile_of(tile + 1))
            if off:
                a = pltpu.roll(a, PAD - off, 1)
            rows32[pl.ds(r * MEMBERS, MEMBERS), :] = jnp.where(lane < NG, a, 0.0)
        for i in range(MEMBERS):
            own[i, x] = rows32[pl.ds(i, PAD, stride=MEMBERS), :].astype(BF)
        return 0

    shifts = [[
        remote(own.at[j, out_span(q)], part.at[j, out_span(q)], sh_send.at[j, q], sh_recv.at[j, q], ahead)
        for q in range(NQ)] for j in range(MEMBERS)]

    def relay_room(j, q):
        return relayed.at[j, pl.ds(0, OUT_GROUPS[q][1])]

    def start_shift(j, q):
        if q not in RELAY_Z:
            shifts[j][q].start()
            return

        @pl.when(last)
        def _():
            remote(own.at[j, out_span(q)], relay_room(j, q), sh_send.at[j, q], re_recv.at[j],
                   {"band": other + 2 * RELAY_Z[q] + 1}).start()

        @pl.when(jnp.logical_not(last))
        def _():
            shifts[j][q].start()

    def handed_on(j, q):
        return remote(relay_room(j, q), part.at[j, out_span(q)], re_send.at[j], sh_recv.at[j, q],
                      {"band": column * side})

    def hand_on(j):
        for q, z in RELAY_Z.items():
            @pl.when(place == 2 * z + 1)
            def _(q=q):
                remote(relay_room(j, q), relay_room(j, q), re_send.at[j], re_recv.at[j], ahead).wait_recv()
                handed_on(j, q).start()

    occ_shift = remote(occ_mine, occ_part, oc_send, oc_recv, ahead)
    for q in range(NQ):
        loads[q].wait()
        lax.fori_loop(OUT_GROUPS[q][0], sum(OUT_GROUPS[q]), unpack, 0)
        if q == 0:
            pl.semaphore_wait(barrier, greetings)
        start_shift(0, q)
    for q in range(NQ):
        start_shift(1, q)
    occ_shift.start()

    lights = [lax.rem(core + j, 2) * (GRID // 2) + 2 * j + core for j in range(MEMBERS)]

    def row_of(j, g):
        return pl.multiple_of(lax.rem(g + 2 * GRID - 1 - lights[j], GRID) * ROWS, ROWS)

    def by_light(is_light, action):
        pl.when(is_light)(functools.partial(action, TILE))
        pl.when(jnp.logical_not(is_light))(functools.partial(action, ROWS))

    kx = square(lax.broadcasted_iota(jnp.int32, (PAD, PAD), 0))
    kz = square(lax.broadcasted_iota(jnp.int32, (PAD, PAD), 1))
    plane_sq = kx + kz
    for j in range(MEMBERS):
        start = row_of(j, me)

        def fill(l, _, j=j, start=start):
            s = plane_sq + square(lax.rem(start + l, NG))
            coul[j, l] = jnp.where(s > 0.5, COULOMB / jnp.maximum(s, 1.0), 0.0)
            return 0
        lax.fori_loop(0, ROWS, fill, 0)
    for j in range(MEMBERS):
        back[j, :, pl.ds(MEMBERS * NG, TILE)] = jnp.zeros((PLANES, TILE, PAD), BF)
    for c in consts:
        c.wait()
    hand_on(0)

    def taken(sem, planes, rows):
        view = send.at[0, pl.ds(0, planes), pl.ds(0, rows)]
        remote(view, view, sem, sem, ahead).wait_recv()

    most, full = (GRID - 2) * ROWS + TILE, (GRID - 1) * ROWS

    def out_sent(j, q):
        @pl.when(me == lights[j])
        def _():
            taken(f_send.at[j, q], OUT_GROUPS[q][1], full)

        @pl.when(me != lights[j])
        def _():
            taken(f_send.at[j, q], OUT_GROUPS[q][1], most)

    def back_sent(j, q):
        by_light(me == lights[j], lambda n: taken(b_send.at[j, q], BACK_GROUPS[q][1], (GRID - 1) * n))

    f_mine, b_mine = {}, {}
    for j in range(MEMBERS):
        for q in range(NQ):
            shifts[j][q].wait_recv()

            def forward(x, _, j=j):
                v = part[j, x]
                d = jnp.concatenate([own[0, x] * v, own[1, x] * v], axis=0)
                t = dot(d, h_ref[...]).astype(BF)
                send[j, x] = dot(second_ref[...], t).astype(BF)
                return 0
            lax.fori_loop(OUT_GROUPS[q][0], sum(OUT_GROUPS[q]), forward, 0, unroll=OUT_GROUPS[q][1])
            if j:
                out_sent(0, q)

            there = pl.ds(me * PLANES + OUT_GROUPS[q][0], OUT_GROUPS[q][1])
            f_mine[j, q] = pltpu.make_async_copy(
                send.at[j, out_span(q), pl.ds(row_of(j, me), ROWS)], got.at[j, there], f_own.at[j, q])
            f_mine[j, q].start()
            for d in range(1, GRID):
                to = lax.rem(me + d, GRID)

                def go(n, j=j, q=q, to=to, there=there):
                    remote(send.at[j, out_span(q), pl.ds(row_of(j, to), n)], got.at[j, there, pl.ds(0, n)],
                           f_send.at[j, q], f_recv.at[j, q], {"grid": to}).start()
                by_light(to == lights[j], go)
            if j == 0 and q == NQ - 1:
                hand_on(1)

    for j in range(MEMBERS):
        for q in range(NQ):
            f_mine[j, q].wait()
            by_light(me == lights[j],
                     lambda n, j=j, q=q: taken(f_recv.at[j, q], OUT_GROUPS[q][1], (GRID - 1) * n))

        def widen(x, _, j=j):
            wide[pl.ds(pl.multiple_of(x * ROWS, ROWS), ROWS), :] = got[j, x].astype(F32)
            return 0
        lax.fori_loop(0, NG, widen, 0, unroll=8)

        def solve(l, _, j=j):
            r = jnp.concatenate(
                [wide[pl.ds(l, PAD, stride=ROWS), :], wide[pl.ds(TILE + l, PAD, stride=ROWS), :]], axis=1)
            f = dot(h_ref[...], r.astype(BF))
            f = (f * jnp.concatenate([coul[j, l], coul[j, TILE + l]], axis=1)).astype(BF)
            g = dot(h_ref[...], f)
            wide2[pl.ds(l, PAD, stride=ROWS), :] = g[:, :PAD]
            wide2[pl.ds(TILE + l, PAD, stride=ROWS), :] = g[:, PAD:]
            return 0
        lax.fori_loop(0, TILE, solve, 0, unroll=4)

        for q in range(NQ):
            begin, planes = BACK_GROUPS[q]

            def narrow(g, _, j=j, begin=begin, planes=planes):
                for x in range(planes):
                    at = g * PLANES + begin + x
                    back_send[j, at] = wide2[pl.ds(pl.multiple_of(at * ROWS, ROWS), ROWS), :].astype(BF)
                return 0
            lax.fori_loop(0, GRID, narrow, 0, unroll=2)
            if j:
                back_sent(0, q)

            def go(n, j=j, q=q, begin=begin, planes=planes):
                here = back.at[j, back_span(q), pl.ds(row_of(j, me), n)]
                pltpu.make_async_copy(
                    back_send.at[j, pl.ds(me * PLANES + begin, planes), pl.ds(0, n)], here, b_own.at[j, q]).start()
                for d in range(1, GRID):
                    to = lax.rem(me + d, GRID)
                    remote(back_send.at[j, pl.ds(to * PLANES + begin, planes), pl.ds(0, n)], here,
                           b_send.at[j, q], b_recv.at[j, q], {"grid": to}).start()
            by_light(me == lights[j], go)

    def came_back(j, q):
        begin, planes = BACK_GROUPS[q]

        def wait(n):
            view = back_send.at[j, pl.ds(me * PLANES + begin, planes), pl.ds(0, n)]
            pltpu.make_async_copy(view, back.at[j, back_span(q), pl.ds(row_of(j, me), n)], b_own.at[j, q]).wait()
            taken(b_recv.at[j, q], planes, full if n == TILE else most)
        by_light(me == lights[j], wait)

    occ_shift.wait_recv()
    returns = [[
        remote(ret.at[j, back_span(q)], ret_got.at[j, back_span(q)], r_send.at[j, q], r_recv.at[j, q], behind)
        for q in range(NQ)] for j in range(MEMBERS)]
    for j in range(MEMBERS):
        for q in range(NQ):
            came_back(j, q)

            def inverse(x, _, j=j):
                u = dot(second_t_ref[...], back[j, x]).astype(BF)
                v = dot(u, h_ref[...])
                v0, v1 = v[:PAD], v[PAD:]
                w = part[j, x].astype(F32) * occ_part[pl.ds(j, 1), :]
                if j == 0:
                    local[0, x] = -(v0 * w)
                    local[1, x] = -(v1 * w)
                else:
                    local[0, x] -= v0 * w
                    local[1, x] -= v1 * w
                s = (v0 * (own[0, x].astype(F32) * occ_mine[pl.ds(0, 1), :])
                     + v1 * (own[1, x].astype(F32) * occ_mine[pl.ds(1, 1), :]))
                ret[j, x] = (-s).astype(BF)
                return 0
            lax.fori_loop(BACK_GROUPS[q][0], sum(BACK_GROUPS[q]), inverse, 0, unroll=BACK_GROUPS[q][1])
            returns[j][q].start()

    def pack(x, _):
        for i in range(MEMBERS):
            rows32[pl.ds(i, PAD, stride=MEMBERS), :] = local[i, x] + ret_got[i, x].astype(F32)
        before = None
        for r in range(NG):
            tile = -(-NG * r // PAD)
            begin = PAD * tile - NG * r
            v = rows32[pl.ds(r * MEMBERS, MEMBERS), :]
            if begin:
                v = pltpu.roll(v, PAD - begin, 1)
            if r % 16:
                t = tile - 1
                z0 = PAD * t - NG * (r - 1)
                xout[x, :, t * PAD:(t + 1) * PAD] = jnp.where(lane < NG - z0, before, v)
            before = v
        xout[x, :, SURFACE - 64:] = before[:, :64]
        return 0

    stores = []
    for q in range(NQ):
        for j in range(MEMBERS):
            returns[j][q].wait_recv()
        lax.fori_loop(BACK_GROUPS[q][0], sum(BACK_GROUPS[q]), pack, 0)
        c = pltpu.make_async_copy(xout.at[back_span(q)], out.at[back_span(q)], out_sem.at[q])
        c.start()
        stores.append(c)

    for c in stores:
        c.wait()
    for c in shifts[0] + shifts[1] + [occ_shift] + returns[0] + returns[1]:
        c.wait_send()
    for q, z in RELAY_Z.items():
        @pl.when(place == 2 * z + 1)
        def _(q=q):
            for j in range(MEMBERS):
                handed_on(j, q).wait_send()
    for q in range(NQ):
        out_sent(1, q)
        back_sent(1, q)


def per_device(bands, occupations):
    h, second, second_t = (jnp.asarray(t) for t in tables())
    dma = pltpu.SemaphoreType.DMA
    hbm = pl.BlockSpec(memory_space=pl.ANY)
    planes_first = bands.transpose(1, 0, 2)
    total = pl.pallas_call(
        kernel,
        out_shape=jax.ShapeDtypeStruct(planes_first.shape, F32),
        in_specs=[hbm, pl.BlockSpec(memory_space=pltpu.SMEM), hbm, hbm, hbm],
        out_specs=hbm,
        scratch_shapes=[
            pltpu.VMEM((PLANES, MEMBERS, SURFACE), F32),
            pltpu.VMEM((PAD * MEMBERS, PAD), F32),
            pltpu.VMEM((MEMBERS, PLANES, PAD, PAD), BF),
            pltpu.VMEM((MEMBERS, PLANES, PAD, PAD), BF),
            pltpu.VMEM((8, PAD), F32),
            pltpu.VMEM((8, PAD), F32),
            pltpu.VMEM((MEMBERS, ROWS, PAD, PAD), F32),
            pltpu.VMEM((MEMBERS, PLANES, GRID * ROWS, PAD), BF),
            pltpu.VMEM((MEMBERS, NG, ROWS, PAD), BF),
            pltpu.VMEM((PAD * ROWS, PAD), F32),
            pltpu.VMEM((PAD * ROWS, PAD), F32),
            pltpu.VMEM((MEMBERS, NG, ROWS, PAD), BF),
            pltpu.VMEM((MEMBERS, PLANES, GRID * ROWS, PAD), BF),
            pltpu.VMEM((MEMBERS, PLANES, PAD, PAD), F32),
            pltpu.VMEM((MEMBERS, PLANES, PAD, PAD), BF),
            pltpu.VMEM((MEMBERS, PLANES, PAD, PAD), BF),
            pltpu.VMEM((PLANES, MEMBERS, SURFACE), F32),
            pltpu.VMEM(h.shape, BF),
            pltpu.VMEM(second.shape, BF),
            pltpu.VMEM(second_t.shape, BF),
            pltpu.VMEM((MEMBERS, RELAY_PLANES, PAD, PAD), BF),
            dma((NQ,)), dma((3,)), dma((NQ,)),
            dma((MEMBERS, NQ)), dma((MEMBERS, NQ)), dma, dma,
            dma((MEMBERS, NQ)), dma((MEMBERS, NQ)), dma((MEMBERS, NQ)),
            dma((MEMBERS, NQ)), dma((MEMBERS, NQ)), dma((MEMBERS, NQ)),
            dma((MEMBERS, NQ)), dma((MEMBERS, NQ)), dma((MEMBERS,)), dma((MEMBERS,)),
        ],
        compiler_params=pltpu.CompilerParams(
            collective_id=0, has_side_effects=True, vmem_limit_bytes=58 * 2**20),
    )(planes_first, occupations, h, second, second_t)
    return total.transpose(1, 0, 2)


def solution(mesh):
    return jax.shard_map(
        per_device,
        mesh=mesh,
        in_specs=(P("band", "grid", None), P("band")),
        out_specs=P("band", "grid", None),
        check_vma=False,
    )
```

time: 76 us -> 70.2 us (0.924)
  Pallas kernels: 73 us -> 67.2 us
    pallas_call x1, Pallas kernels: 73 us -> 67.2 us  [per_device(): pl.pallas_call(kernel, out_shape=jax.ShapeDtypeStruct(planes_first.shape,...]
where the time goes in v3:
time: 70.2 us; the launch traced here: 70 us
  Pallas kernels  67.2 us (96%)
  local copies, waits for them, and re-layouts  2.78 us (4%)
    pallas_call x1, Pallas kernels, per_device(): pl.pallas_call(kernel, out_shape=jax.ShapeDtypeStruct(planes_first.shape,...  67.2 us
    unnamed x1, local copies, waits for them, and re-layouts  2.78 us

profile of v3, /device:TPU:24, one launch (start us, length us, event | category | flops | bytes accessed | tf_op | source)
XLA Modules:
  0.0 70.0 jit_solution(17788211071957282123)
XLA Ops:
  0.0 67.2 %shard_map.55 = f32[15,2,14400]{2,1,0:T(2,128)} custom-call(f32[15,2,14400]{2,1,0:T(2,128)} %bitcast.3, f32[2]{0:T(128)} %occ.1, bf16[128,128]{1,0:T(8,128)(2,1)} %constant.6.clone.h_hbm, bf16[256,256]{1,0:T(8,128)(2,1)} %constant.7.clone.second_hbm, bf16[256,256]{1,0:T(8,128)(2,1)} %constant.8.clone.second_t_hbm), custom_call_target="tpu_custom_call" | custom-call | tf_op jit(solution)/shard_map/pallas_call | solution.py:387
  67.2 2.8 %copy.7 = f32[2,15,14400]{2,0,1:T(2,128)} copy(f32[2,15,14400]{2,0,1:T(2,128)} %bitcast.2) | data formatting | bytes 3456000

commit v4 on v3

--- a/solution.py
+++ b/solution.py
@@ -18,11 +18,14 @@
 MEMBERS = 2
 ROWS = 32
 TILE = 16
-OUT_GROUPS = ((0, 5), (5, 5), (10, 5))
-BACK_GROUPS = ((0, 5), (5, 5), (10, 5))
+OUT_GROUPS = ((0, 3), (3, 5), (8, 7))
+BACK_GROUPS = ((0, 7), (7, 5), (12, 3))
 NQ = len(OUT_GROUPS)
-RELAY_Z = {1: 6, 2: 5}
+RELAY_Z = {1: 3, 2: 2}
+HAND_ON = {(0, 2): 0, (1, 0): 1}
+RETURN_Z = {0: 6, 1: 5, 2: 4}
 RELAY_PLANES = max(OUT_GROUPS[q][1] for q in RELAY_Z)
+RETURN_PLANES = max(BACK_GROUPS[q][1] for q in RETURN_Z)
 SURFACE = NG * NG
 MESH = pl.DeviceIdType.MESH
 BF = jnp.bfloat16
@@ -57,9 +60,9 @@
 
 def kernel(bands, occ, h_hbm, second_hbm, second_t_hbm, out,
            xin, rows32, own, part, occ_mine, occ_part, coul, send, got, wide, wide2,
-           back_send, back, local, ret, ret_got, xout, h_ref, second_ref, second_t_ref, relayed,
+           back_send, back, local, ret, ret_got, xout, h_ref, second_ref, second_t_ref, relayed, returned,
            in_sem, c_sem, out_sem, sh_send, sh_recv, oc_send, oc_recv, f_send, f_recv, f_own,
-           b_send, b_recv, b_own, r_send, r_recv, re_send, re_recv):
+           b_send, b_recv, b_own, r_send, r_recv, re_send, re_recv, rr_send, rr_recv):
     me_b = lax.axis_index("band")
     me = lax.axis_index("grid")
     groups = lax.axis_size("band")
@@ -102,16 +105,20 @@
         greet({"grid": lax.rem(me + d, GRID)})
     greet(ahead)
     greet(behind)
-    greetings = GRID + 1 + jnp.where(last, len(RELAY_Z), 0)
-    for z in RELAY_Z.values():
-        @pl.when(place == 2 * z + 1)
-        def _():
-            greet({"band": other + side - 1})
-
-        @pl.when(first)
-        def _(z=z):
-            greet({"band": column * side + 2 * z + 1})
-        greetings += (place == 2 * z + 1).astype(jnp.int32)
+    greetings = GRID + 1
+    for is_source, source, is_target, stops in (
+            (last, side - 1, first, [2 * z + 1 for z in RELAY_Z.values()]),
+            (first, 0, last, [2 * z for z in RETURN_Z.values()])):
+        for stop in stops:
+            @pl.when(place == stop)
+            def _(source=source):
+                greet({"band": other + source})
+
+            @pl.when(is_target)
+            def _(stop=stop):
+                greet({"band": column * side + stop})
+            greetings += (place == stop).astype(jnp.int32)
+        greetings += jnp.where(is_source, len(stops), 0)
 
     lane = lax.broadcasted_iota(jnp.int32, (MEMBERS, PAD), 1)
     rows32[pl.ds(NG * MEMBERS, 8 * MEMBERS), :] = jnp.zeros((8 * MEMBERS, PAD), F32)
@@ -175,6 +182,34 @@
                 remote(relay_room(j, q), relay_room(j, q), re_send.at[j], re_recv.at[j], ahead).wait_recv()
                 handed_on(j, q).start()
 
+    def start_return(j, q):
+        if j or q not in RETURN_Z:
+            returns[j][q].start()
+            return
+
+        @pl.when(first)
+        def _():
+            remote(ret.at[j, back_span(q)], return_room(q), r_send.at[j, q], rr_recv,
+                   {"band": other + 2 * RETURN_Z[q]}).start()
+
+        @pl.when(jnp.logical_not(first))
+        def _():
+            returns[j][q].start()
+
+    def return_room(q):
+        return returned.at[pl.ds(0, BACK_GROUPS[q][1])]
+
+    def handed_back(q):
+        return remote(return_room(q), ret_got.at[0, back_span(q)], rr_send, r_recv.at[0, q],
+                      {"band": column * side + side - 1})
+
+    def hand_back():
+        for q, z in RETURN_Z.items():
+            @pl.when(place == 2 * z)
+            def _(q=q):
+                remote(return_room(q), return_room(q), rr_send, rr_recv, ahead).wait_recv()
+                handed_back(q).start()
+
     occ_shift = remote(occ_mine, occ_part, oc_send, oc_recv, ahead)
     for q in range(NQ):
         loads[q].wait()
@@ -195,22 +230,8 @@
         pl.when(is_light)(functools.partial(action, TILE))
         pl.when(jnp.logical_not(is_light))(functools.partial(action, ROWS))
 
-    kx = square(lax.broadcasted_iota(jnp.int32, (PAD, PAD), 0))
-    kz = square(lax.broadcasted_iota(jnp.int32, (PAD, PAD), 1))
-    plane_sq = kx + kz
-    for j in range(MEMBERS):
-        start = row_of(j, me)
-
-        def fill(l, _, j=j, start=start):
-            s = plane_sq + square(lax.rem(start + l, NG))
-            coul[j, l] = jnp.where(s > 0.5, COULOMB / jnp.maximum(s, 1.0), 0.0)
-            return 0
-        lax.fori_loop(0, ROWS, fill, 0)
-    for j in range(MEMBERS):
-        back[j, :, pl.ds(MEMBERS * NG, TILE)] = jnp.zeros((PLANES, TILE, PAD), BF)
     for c in consts:
         c.wait()
-    hand_on(0)
 
     def taken(sem, planes, rows):
         view = send.at[0, pl.ds(0, planes), pl.ds(0, rows)]
@@ -256,9 +277,22 @@
                     remote(send.at[j, out_span(q), pl.ds(row_of(j, to), n)], got.at[j, there, pl.ds(0, n)],
                            f_send.at[j, q], f_recv.at[j, q], {"grid": to}).start()
                 by_light(to == lights[j], go)
-            if j == 0 and q == NQ - 1:
-                hand_on(1)
-
+            if (j, q) in HAND_ON:
+                hand_on(HAND_ON[j, q])
+
+    kx = square(lax.broadcasted_iota(jnp.int32, (PAD, PAD), 0))
+    kz = square(lax.broadcasted_iota(jnp.int32, (PAD, PAD), 1))
+    plane_sq = kx + kz
+    for j in range(MEMBERS):
+        start = row_of(j, me)
+
+        def fill(l, _, j=j, start=start):
+            s = plane_sq + square(lax.rem(start + l, NG))
+            coul[j, l] = jnp.where(s > 0.5, COULOMB / jnp.maximum(s, 1.0), 0.0)
+            return 0
+        lax.fori_loop(0, ROWS, fill, 0)
+    for j in range(MEMBERS):
+        back[j, :, pl.ds(MEMBERS * NG, TILE)] = jnp.zeros((PLANES, TILE, PAD), BF)
     for j in range(MEMBERS):
         for q in range(NQ):
             f_mine[j, q].wait()
@@ -336,7 +370,9 @@
                 ret[j, x] = (-s).astype(BF)
                 return 0
             lax.fori_loop(BACK_GROUPS[q][0], sum(BACK_GROUPS[q]), inverse, 0, unroll=BACK_GROUPS[q][1])
-            returns[j][q].start()
+            start_return(j, q)
+            if j and q == 1:
+                hand_back()
 
     def pack(x, _):
         for i in range(MEMBERS):
@@ -374,6 +410,10 @@
         def _(q=q):
             for j in range(MEMBERS):
                 handed_on(j, q).wait_send()
+    for q, z in RETURN_Z.items():
+        @pl.when(place == 2 * z)
+        def _(q=q):
+            handed_back(q).wait_send()
     for q in range(NQ):
         out_sent(1, q)
         back_sent(1, q)
@@ -411,11 +451,12 @@
             pltpu.VMEM(second.shape, BF),
             pltpu.VMEM(second_t.shape, BF),
             pltpu.VMEM((MEMBERS, RELAY_PLANES, PAD, PAD), BF),
+            pltpu.VMEM((RETURN_PLANES, PAD, PAD), BF),
             dma((NQ,)), dma((3,)), dma((NQ,)),
             dma((MEMBERS, NQ)), dma((MEMBERS, NQ)), dma, dma,
             dma((MEMBERS, NQ)), dma((MEMBERS, NQ)), dma((MEMBERS, NQ)),
             dma((MEMBERS, NQ)), dma((MEMBERS, NQ)), dma((MEMBERS, NQ)),
-            dma((MEMBERS, NQ)), dma((MEMBERS, NQ)), dma((MEMBERS,)), dma((MEMBERS,)),
+            dma((MEMBERS, NQ)), dma((MEMBERS, NQ)), dma((MEMBERS,)), dma((MEMBERS,)), dma, dma,
         ],
         compiler_params=pltpu.CompilerParams(
             collective_id=0, has_side_effects=True, vmem_limit_bytes=58 * 2**20),

time: 70.2 us -> 68.4 us (0.974)
  Pallas kernels: 67.2 us -> 64.9 us
    pallas_call x1, Pallas kernels: 67.2 us -> 64.9 us  [per_device(): pl.pallas_call(kernel, out_shape=jax.ShapeDtypeStruct(planes_first.shape,...]
where the time goes in v4:
time: 68.4 us; the launch traced here: 67.7 us
  Pallas kernels  64.9 us (95%)
  local copies, waits for them, and re-layouts  2.78 us (4%)
    pallas_call x1, Pallas kernels, per_device(): pl.pallas_call(kernel, out_shape=jax.ShapeDtypeStruct(planes_first.shape,...  64.9 us
    unnamed x1, local copies, waits for them, and re-layouts  2.78 us

profile of v4, /device:TPU:24, one launch (start us, length us, event | category | flops | bytes accessed | tf_op | source)
XLA Modules:
  0.0 67.7 jit_solution(7577685836941654753)
XLA Ops:
  0.0 64.9 %shard_map.55 = f32[15,2,14400]{2,1,0:T(2,128)} custom-call(f32[15,2,14400]{2,1,0:T(2,128)} %bitcast.3, f32[2]{0:T(128)} %occ.1, bf16[128,128]{1,0:T(8,128)(2,1)} %constant.6.clone.h_hbm, bf16[256,256]{1,0:T(8,128)(2,1)} %constant.7.clone.second_hbm, bf16[256,256]{1,0:T(8,128)(2,1)} %constant.8.clone.second_t_hbm), custom_call_target="tpu_custom_call" | custom-call | tf_op jit(solution)/shard_map/pallas_call | solution.py:427
  64.9 2.8 %copy.7 = f32[2,15,14400]{2,0,1:T(2,128)} copy(f32[2,15,14400]{2,0,1:T(2,128)} %bitcast.2) | data formatting | bytes 3456000

commit v5 on v4

--- a/solution.py
+++ b/solution.py
@@ -21,10 +21,10 @@
 OUT_GROUPS = ((0, 3), (3, 5), (8, 7))
 BACK_GROUPS = ((0, 7), (7, 5), (12, 3))
 NQ = len(OUT_GROUPS)
-RELAY_Z = {1: 3, 2: 2}
-HAND_ON = {(0, 2): 0, (1, 0): 1}
-RETURN_Z = {0: 6, 1: 5, 2: 4}
-RELAY_PLANES = max(OUT_GROUPS[q][1] for q in RELAY_Z)
+RELAY_Z = {(0, 1): 3, (0, 2): 2, (1, 1): 4, (1, 2): 1}
+HAND_ON = {(0, 2): 0, (1, 1): 1}
+RETURN_Z = {0: 6, 1: 5}
+RELAY_PLANES = max(OUT_GROUPS[q][1] for _, q in RELAY_Z)
 RETURN_PLANES = max(BACK_GROUPS[q][1] for q in RETURN_Z)
 SURFACE = NG * NG
 MESH = pl.DeviceIdType.MESH
@@ -154,33 +154,34 @@
         remote(own.at[j, out_span(q)], part.at[j, out_span(q)], sh_send.at[j, q], sh_recv.at[j, q], ahead)
         for q in range(NQ)] for j in range(MEMBERS)]
 
-    def relay_room(j, q):
-        return relayed.at[j, pl.ds(0, OUT_GROUPS[q][1])]
+    def relay_room(q):
+        return relayed.at[pl.ds(0, OUT_GROUPS[q][1])]
 
     def start_shift(j, q):
-        if q not in RELAY_Z:
+        if (j, q) not in RELAY_Z:
             shifts[j][q].start()
             return
 
         @pl.when(last)
         def _():
-            remote(own.at[j, out_span(q)], relay_room(j, q), sh_send.at[j, q], re_recv.at[j],
-                   {"band": other + 2 * RELAY_Z[q] + 1}).start()
+            remote(own.at[j, out_span(q)], relay_room(q), sh_send.at[j, q], re_recv,
+                   {"band": other + 2 * RELAY_Z[j, q] + 1}).start()
 
         @pl.when(jnp.logical_not(last))
         def _():
             shifts[j][q].start()
 
     def handed_on(j, q):
-        return remote(relay_room(j, q), part.at[j, out_span(q)], re_send.at[j], sh_recv.at[j, q],
+        return remote(relay_room(q), part.at[j, out_span(q)], re_send, sh_recv.at[j, q],
                       {"band": column * side})
 
-    def hand_on(j):
-        for q, z in RELAY_Z.items():
-            @pl.when(place == 2 * z + 1)
-            def _(q=q):
-                remote(relay_room(j, q), relay_room(j, q), re_send.at[j], re_recv.at[j], ahead).wait_recv()
-                handed_on(j, q).start()
+    def hand_on(wanted):
+        for (j, q), z in RELAY_Z.items():
+            if j == wanted:
+                @pl.when(place == 2 * z + 1)
+                def _(j=j, q=q):
+                    remote(relay_room(q), relay_room(q), re_send, re_recv, ahead).wait_recv()
+                    handed_on(j, q).start()
 
     def start_return(j, q):
         if j or q not in RETURN_Z:
@@ -405,11 +406,10 @@
         c.wait()
     for c in shifts[0] + shifts[1] + [occ_shift] + returns[0] + returns[1]:
         c.wait_send()
-    for q, z in RELAY_Z.items():
+    for (j, q), z in RELAY_Z.items():
         @pl.when(place == 2 * z + 1)
-        def _(q=q):
-            for j in range(MEMBERS):
-                handed_on(j, q).wait_send()
+        def _(j=j, q=q):
+            handed_on(j, q).wait_send()
     for q, z in RETURN_Z.items():
         @pl.when(place == 2 * z)
         def _(q=q):
@@ -417,6 +417,20 @@
     for q in range(NQ):
         out_sent(1, q)
         back_sent(1, q)
+
+
+def pass_on(steps, src, dst, held, in_sem, out_sem):
+    planes = PLANES // steps
+    spans = [pl.ds(n * planes, planes) for n in range(steps)]
+    loads = [pltpu.make_async_copy(src.at[p], held.at[p], in_sem.at[n]) for n, p in enumerate(spans)]
+    stores = [pltpu.make_async_copy(held.at[p], dst.at[p], out_sem.at[n]) for n, p in enumerate(spans)]
+    for c in loads:
+        c.start()
+    for load, store in zip(loads, stores):
+        load.wait()
+        store.start()
+    for c in stores:
+        c.wait()
 
 
 def per_device(bands, occupations):
@@ -450,17 +464,26 @@
             pltpu.VMEM(h.shape, BF),
             pltpu.VMEM(second.shape, BF),
             pltpu.VMEM(second_t.shape, BF),
-            pltpu.VMEM((MEMBERS, RELAY_PLANES, PAD, PAD), BF),
+            pltpu.VMEM((RELAY_PLANES, PAD, PAD), BF),
             pltpu.VMEM((RETURN_PLANES, PAD, PAD), BF),
             dma((NQ,)), dma((3,)), dma((NQ,)),
             dma((MEMBERS, NQ)), dma((MEMBERS, NQ)), dma, dma,
             dma((MEMBERS, NQ)), dma((MEMBERS, NQ)), dma((MEMBERS, NQ)),
             dma((MEMBERS, NQ)), dma((MEMBERS, NQ)), dma((MEMBERS, NQ)),
-            dma((MEMBERS, NQ)), dma((MEMBERS, NQ)), dma((MEMBERS,)), dma((MEMBERS,)), dma, dma,
+            dma((MEMBERS, NQ)), dma((MEMBERS, NQ)), dma, dma, dma, dma,
         ],
         compiler_params=pltpu.CompilerParams(
             collective_id=0, has_side_effects=True, vmem_limit_bytes=58 * 2**20),
     )(planes_first, occupations, h, second, second_t)
+    steps = 5
+    total = pl.pallas_call(
+        functools.partial(pass_on, steps),
+        out_shape=jax.ShapeDtypeStruct(planes_first.shape, F32),
+        in_specs=[hbm],
+        out_specs=hbm,
+        scratch_shapes=[pltpu.VMEM(planes_first.shape, F32), dma((steps,)), dma((steps,))],
+        compiler_params=pltpu.CompilerParams(vmem_limit_bytes=58 * 2**20),
+    )(total)
     return total.transpose(1, 0, 2)
 
 

time: 68.4 us -> 67.1 us (0.981)
  the two profiles are of different devices: /device:TPU:24 before, /device:TPU:251 now
where the time goes in v5:
time: 67.1 us; the launch traced here: 66.9 us
  Pallas kernels  66.9 us (100%)
    pallas_call x1, Pallas kernels, per_device(): pl.pallas_call(kernel, out_shape=jax.ShapeDtypeStruct(planes_first.shape,...  64.7 us
    pallas_call x1, Pallas kernels, per_device(): pl.pallas_call(functools.partial(pass_on, steps), out_shape=jax.ShapeDtyp...  2.25 us

profile of v5, /device:TPU:251, one launch (start us, length us, event | category | flops | bytes accessed | tf_op | source)
XLA Modules:
  0.0 66.9 jit_solution(16750093064313124394)
XLA Ops:
  0.0 64.7 %shard_map.55.src = f32[15,2,14400]{2,1,0:T(2,128)} custom-call(f32[15,2,14400]{2,1,0:T(2,128)} %bitcast.2, f32[2]{0:T(128)} %occ.1, bf16[128,128]{1,0:T(8,128)(2,1)} %constant.6.clone.h_hbm, bf16[256,256]{1,0:T(8,128)(2,1)} %constant.7.clone.second_hbm, bf16[256,256]{1,0:T(8,128)(2,1)} %constant.8.clone.second_t_hbm), custom_call_target="tpu_custom_call" | custom-call | tf_op jit(solution)/shard_map/pallas_call | solution.py:441
  64.7 2.3 %shard_map.56 = f32[15,2,14400]{2,1,0:T(2,128)} custom-call(f32[15,2,14400]{2,1,0:T(2,128)} %shard_map.55.src), custom_call_target="tpu_custom_call" | custom-call | tf_op jit(solution)/shard_map/pallas_call | solution.py:479

commit v6 on v5

--- a/solution.py
+++ b/solution.py
@@ -21,6 +21,7 @@
 OUT_GROUPS = ((0, 3), (3, 5), (8, 7))
 BACK_GROUPS = ((0, 7), (7, 5), (12, 3))
 NQ = len(OUT_GROUPS)
+EARLY = 2
 RELAY_Z = {(0, 1): 3, (0, 2): 2, (1, 1): 4, (1, 2): 1}
 HAND_ON = {(0, 2): 0, (1, 1): 1}
 RETURN_Z = {0: 6, 1: 5}
@@ -145,7 +146,7 @@
                 a = jnp.where(lane >= off, a, tile_of(tile + 1))
             if off:
                 a = pltpu.roll(a, PAD - off, 1)
-            rows32[pl.ds(r * MEMBERS, MEMBERS), :] = jnp.where(lane < NG, a, 0.0)
+            rows32[pl.ds(r * MEMBERS, MEMBERS), :] = a
         for i in range(MEMBERS):
             own[i, x] = rows32[pl.ds(i, PAD, stride=MEMBERS), :].astype(BF)
         return 0
@@ -212,74 +213,79 @@
                 handed_back(q).start()
 
     occ_shift = remote(occ_mine, occ_part, oc_send, oc_recv, ahead)
+    lights = [lax.rem(core + j, 2) * (GRID // 2) + 2 * j + core for j in range(MEMBERS)]
+
+    def row_of(j, g):
+        return pl.multiple_of(lax.rem(g + 2 * GRID - 1 - lights[j], GRID) * ROWS, ROWS)
+
+    def by_light(is_light, action):
+        pl.when(is_light)(functools.partial(action, TILE))
+        pl.when(jnp.logical_not(is_light))(functools.partial(action, ROWS))
+
+    def taken(sem, planes, rows):
+        view = send.at[0, pl.ds(0, planes), pl.ds(0, rows)]
+        remote(view, view, sem, sem, ahead).wait_recv()
+
+    most, full = (GRID - 2) * ROWS + TILE, (GRID - 1) * ROWS
+
+    def out_sent(j, q):
+        @pl.when(me == lights[j])
+        def _():
+            taken(f_send.at[j, q], OUT_GROUPS[q][1], full)
+
+        @pl.when(me != lights[j])
+        def _():
+            taken(f_send.at[j, q], OUT_GROUPS[q][1], most)
+
+    def back_sent(j, q):
+        by_light(me == lights[j], lambda n: taken(b_send.at[j, q], BACK_GROUPS[q][1], (GRID - 1) * n))
+
+    f_mine = {}
+
+    def advance(j, q):
+        shifts[j][q].wait_recv()
+
+        def forward(x, _):
+            v = part[j, x]
+            d = jnp.concatenate([own[0, x] * v, own[1, x] * v], axis=0)
+            t = dot(d, h_ref[...]).astype(BF)
+            send[j, x] = dot(second_ref[...], t).astype(BF)
+            return 0
+        lax.fori_loop(OUT_GROUPS[q][0], sum(OUT_GROUPS[q]), forward, 0, unroll=OUT_GROUPS[q][1])
+        if j:
+            out_sent(0, q)
+
+        there = pl.ds(me * PLANES + OUT_GROUPS[q][0], OUT_GROUPS[q][1])
+        f_mine[j, q] = pltpu.make_async_copy(
+            send.at[j, out_span(q), pl.ds(row_of(j, me), ROWS)], got.at[j, there], f_own.at[j, q])
+        f_mine[j, q].start()
+        for d in range(1, GRID):
+            to = lax.rem(me + d, GRID)
+
+            def go(n, to=to):
+                remote(send.at[j, out_span(q), pl.ds(row_of(j, to), n)], got.at[j, there, pl.ds(0, n)],
+                       f_send.at[j, q], f_recv.at[j, q], {"grid": to}).start()
+            by_light(to == lights[j], go)
+        if (j, q) in HAND_ON:
+            hand_on(HAND_ON[j, q])
+
     for q in range(NQ):
         loads[q].wait()
         lax.fori_loop(OUT_GROUPS[q][0], sum(OUT_GROUPS[q]), unpack, 0)
         if q == 0:
             pl.semaphore_wait(barrier, greetings)
         start_shift(0, q)
+        if q == EARLY:
+            for c in consts:
+                c.wait()
+            advance(0, 0)
     for q in range(NQ):
         start_shift(1, q)
     occ_shift.start()
-
-    lights = [lax.rem(core + j, 2) * (GRID // 2) + 2 * j + core for j in range(MEMBERS)]
-
-    def row_of(j, g):
-        return pl.multiple_of(lax.rem(g + 2 * GRID - 1 - lights[j], GRID) * ROWS, ROWS)
-
-    def by_light(is_light, action):
-        pl.when(is_light)(functools.partial(action, TILE))
-        pl.when(jnp.logical_not(is_light))(functools.partial(action, ROWS))
-
-    for c in consts:
-        c.wait()
-
-    def taken(sem, planes, rows):
-        view = send.at[0, pl.ds(0, planes), pl.ds(0, rows)]
-        remote(view, view, sem, sem, ahead).wait_recv()
-
-    most, full = (GRID - 2) * ROWS + TILE, (GRID - 1) * ROWS
-
-    def out_sent(j, q):
-        @pl.when(me == lights[j])
-        def _():
-            taken(f_send.at[j, q], OUT_GROUPS[q][1], full)
-
-        @pl.when(me != lights[j])
-        def _():
-            taken(f_send.at[j, q], OUT_GROUPS[q][1], most)
-
-    def back_sent(j, q):
-        by_light(me == lights[j], lambda n: taken(b_send.at[j, q], BACK_GROUPS[q][1], (GRID - 1) * n))
-
-    f_mine, b_mine = {}, {}
     for j in range(MEMBERS):
         for q in range(NQ):
-            shifts[j][q].wait_recv()
-
-            def forward(x, _, j=j):
-                v = part[j, x]
-                d = jnp.concatenate([own[0, x] * v, own[1, x] * v], axis=0)
-                t = dot(d, h_ref[...]).astype(BF)
-                send[j, x] = dot(second_ref[...], t).astype(BF)
-                return 0
-            lax.fori_loop(OUT_GROUPS[q][0], sum(OUT_GROUPS[q]), forward, 0, unroll=OUT_GROUPS[q][1])
-            if j:
-                out_sent(0, q)
-
-            there = pl.ds(me * PLANES + OUT_GROUPS[q][0], OUT_GROUPS[q][1])
-            f_mine[j, q] = pltpu.make_async_copy(
-                send.at[j, out_span(q), pl.ds(row_of(j, me), ROWS)], got.at[j, there], f_own.at[j, q])
-            f_mine[j, q].start()
-            for d in range(1, GRID):
-                to = lax.rem(me + d, GRID)
-
-                def go(n, j=j, q=q, to=to, there=there):
-                    remote(send.at[j, out_span(q), pl.ds(row_of(j, to), n)], got.at[j, there, pl.ds(0, n)],
-                           f_send.at[j, q], f_recv.at[j, q], {"grid": to}).start()
-                by_light(to == lights[j], go)
-            if (j, q) in HAND_ON:
-                hand_on(HAND_ON[j, q])
+            if j or q:
+                advance(j, q)
 
     kx = square(lax.broadcasted_iota(jnp.int32, (PAD, PAD), 0))
     kz = square(lax.broadcasted_iota(jnp.int32, (PAD, PAD), 1))

time: 67.1 us -> 67 us (level)
  the two profiles are of different devices: /device:TPU:251 before, /device:TPU:217 now
where the time goes in v6:
time: 67 us; the launch traced here: 66.9 us
  Pallas kernels  66.9 us (100%)
    pallas_call x1, Pallas kernels, per_device(): pl.pallas_call(kernel, out_shape=jax.ShapeDtypeStruct(planes_first.shape,...  64.6 us
    pallas_call x1, Pallas kernels, per_device(): pl.pallas_call(functools.partial(pass_on, steps), out_shape=jax.ShapeDtyp...  2.25 us

profile of v6, /device:TPU:217, one launch (start us, length us, event | category | flops | bytes accessed | tf_op | source)
XLA Modules:
  0.0 66.9 jit_solution(7613455216651804490)
XLA Ops:
  0.0 64.6 %shard_map.55.src = f32[15,2,14400]{2,1,0:T(2,128)} custom-call(f32[15,2,14400]{2,1,0:T(2,128)} %bitcast.2, f32[2]{0:T(128)} %occ.1, bf16[128,128]{1,0:T(8,128)(2,1)} %constant.6.clone.h_hbm, bf16[256,256]{1,0:T(8,128)(2,1)} %constant.7.clone.second_hbm, bf16[256,256]{1,0:T(8,128)(2,1)} %constant.8.clone.second_t_hbm), custom_call_target="tpu_custom_call" | custom-call | tf_op jit(solution)/shard_map/pallas_call | solution.py:447
  64.7 2.3 %shard_map.56 = f32[15,2,14400]{2,1,0:T(2,128)} custom-call(f32[15,2,14400]{2,1,0:T(2,128)} %shard_map.55.src), custom_call_target="tpu_custom_call" | custom-call | tf_op jit(solution)/shard_map/pallas_call | solution.py:485

commit v7 on v6

--- a/solution.py
+++ b/solution.py
@@ -271,7 +271,7 @@
 
     for q in range(NQ):
         loads[q].wait()
-        lax.fori_loop(OUT_GROUPS[q][0], sum(OUT_GROUPS[q]), unpack, 0)
+        lax.fori_loop(OUT_GROUPS[q][0], sum(OUT_GROUPS[q]), unpack, 0, unroll=OUT_GROUPS[q][1])
         if q == 0:
             pl.semaphore_wait(barrier, greetings)
         start_shift(0, q)
@@ -403,7 +403,7 @@
     for q in range(NQ):
         for j in range(MEMBERS):
             returns[j][q].wait_recv()
-        lax.fori_loop(BACK_GROUPS[q][0], sum(BACK_GROUPS[q]), pack, 0)
+        lax.fori_loop(BACK_GROUPS[q][0], sum(BACK_GROUPS[q]), pack, 0, unroll=BACK_GROUPS[q][1])
         c = pltpu.make_async_copy(xout.at[back_span(q)], out.at[back_span(q)], out_sem.at[q])
         c.start()
         stores.append(c)

time: 67 us -> 65.6 us (0.979)
  the two profiles are of different devices: /device:TPU:217 before, /device:TPU:24 now
where the time goes in v7:
time: 65.6 us; the launch traced here: 65.5 us
  Pallas kernels  65.3 us (100%)
    pallas_call x1, Pallas kernels, per_device(): pl.pallas_call(kernel, out_shape=jax.ShapeDtypeStruct(planes_first.shape,...  63.1 us
    pallas_call x1, Pallas kernels, per_device(): pl.pallas_call(functools.partial(pass_on, steps), out_shape=jax.ShapeDtyp...  2.25 us

profile of v7, /device:TPU:24, one launch (start us, length us, event | category | flops | bytes accessed | tf_op | source)
XLA Modules:
  0.0 65.5 jit_solution(12989166233212237809)
XLA Ops:
  0.0 63.1 %shard_map.55.src = f32[15,2,14400]{2,1,0:T(2,128)} custom-call(f32[15,2,14400]{2,1,0:T(2,128)} %bitcast.2, f32[2]{0:T(128)} %occ.1, bf16[128,128]{1,0:T(8,128)(2,1)} %constant.6.clone.h_hbm, bf16[256,256]{1,0:T(8,128)(2,1)} %constant.7.clone.second_hbm, bf16[256,256]{1,0:T(8,128)(2,1)} %constant.8.clone.second_t_hbm), custom_call_target="tpu_custom_call" | custom-call | tf_op jit(solution)/shard_map/pallas_call | solution.py:447
  63.1 2.3 %shard_map.56 = f32[15,2,14400]{2,1,0:T(2,128)} custom-call(f32[15,2,14400]{2,1,0:T(2,128)} %shard_map.55.src), custom_call_target="tpu_custom_call" | custom-call | tf_op jit(solution)/shard_map/pallas_call | solution.py:485
